TPU v7x, 128 devices: a whole 4x4x4 slice. The times are simulated.
128 devices in a mesh: blk: 32 (over z, y, x_hi), img: 4 (over x_lo, core).
Axes of the slice: x: 4 (x_hi: 2, x_lo: 2; x = x_hi * 2 + x_lo), y: 4, z: 4, core: 2. Of those that a mesh axis runs over, the one named last changes fastest.
Arguments:
- images: bfloat16 [16384, 1152], P(('blk', 'img')), may hold values from -0.1875 to 0.1875
- texts: bfloat16 [16384, 1152], P(('blk', 'img')), may hold values from -0.1875 to 0.1875
- cache: bfloat16 [16384, 1152], P(('blk', 'img')), may hold values from -0.1875 to 0.1875
- mate_owner: int32 [16384, 4], P(('blk', 'img')), may hold values from 0 to 127, all different within a row; in each aligned block of 128 rows (0 to 127, 128 to 255, ...) at most 8 rows name the same one
- mate_row: int32 [16384, 4], P(('blk', 'img')), may hold values from 0 to 127
- mate_count: int32 [16384], P(('blk', 'img')), may hold values from 1 to 4
- log_scale: float32 [1], replicated, may hold values from 1.8 to 2.6
- bias: float32 [1], replicated, may hold values from -6 to -2
Outputs:
- image_grad: float32 [16384, 1152], P(('blk', 'img'))
- text_grad: float32 [16384, 1152], P(('blk', 'img'))
- cache_grad: float32 [16384, 1152], P(('blk', 'img'))
Inputs may be any that keep to these rules, and one draw needn't show every extreme that they name: `mate_owner`: among the 4 entries of the 128 rows of one device, each owner is named at most 8 times, and some device names some owner exactly 8 times; within a row the owners differ.
All inputs are finite; a program needn't handle non-finite values.
Results may differ from a plain program's by a relative error of at most 0.0034.
Values may be sent and summed in bfloat16 or wider, within the bound.
A program may use at most 128 MiB of HBM per device.

v0:
```python
import jax
import jax.numpy as jnp
from jax import lax
from jax.sharding import PartitionSpec as P


def shards(images, texts, cache, mate_owner, mate_row, mate_count, log_scale, bias):
    scale = jnp.exp(log_scale[0])
    offset = bias[0]
    rows_dev, width = images.shape
    mates = mate_owner.shape[1]
    n_img = lax.axis_size("img")
    n_blk = lax.axis_size("blk")
    owners = n_img * n_blk
    cap = max(2, 2 * rows_dev * mates // owners)
    blk_idx = lax.axis_index("blk")
    img_idx = lax.axis_index("img")
    img_all = lax.all_gather(images, "img", axis=0, tiled=True)
    group_rows = img_all.shape[0]
    group_ids = blk_idx * n_img * rows_dev + jnp.arange(group_rows, dtype=jnp.int32)

    def coefficients(left, right, left_ids, right_ids):
        logits = scale * jnp.dot(left, right.T, preferred_element_type=jnp.float32) + offset
        same = (left_ids[:, None] == right_ids[None, :]).astype(jnp.float32)
        return (scale * (jax.nn.sigmoid(logits) - same)).astype(jnp.bfloat16)

    def column_ids(count):
        where_at = jnp.arange(count, dtype=jnp.int32)
        return (where_at // rows_dev * n_img + img_idx) * rows_dev + where_at % rows_dev

    piece = lax.all_gather(texts, "blk", axis=0, tiled=True)
    coeff = coefficients(img_all, piece, group_ids, column_ids(piece.shape[0]))
    partial_img = jnp.dot(coeff, piece, preferred_element_type=jnp.float32)
    txt_all = lax.all_gather(texts, "img", axis=0, tiled=True)
    piece = lax.all_gather(images, "blk", axis=0, tiled=True)
    coeff = coefficients(txt_all, piece, group_ids, column_ids(piece.shape[0]))
    partial_txt = jnp.dot(coeff, piece, preferred_element_type=jnp.float32)
    text_grad = lax.psum_scatter(partial_txt, "img", scatter_dimension=0, tiled=True)
    image_grad = lax.psum_scatter(partial_img, "img", scatter_dimension=0, tiled=True)
    owner_flat = mate_owner.reshape(-1)
    row_flat = mate_row.reshape(-1)
    owner_hits = (owner_flat[:, None] == jnp.arange(owners, dtype=jnp.int32)[None, :]).astype(
        jnp.int32
    )
    rank = jnp.sum((jnp.cumsum(owner_hits, axis=0) - owner_hits) * owner_hits, axis=1)
    slot = owner_flat * cap + rank
    table = jnp.zeros((owners * cap,), jnp.int32).at[slot].set(row_flat).reshape(owners, cap)
    asked = lax.all_to_all(table, ("blk", "img"), split_axis=0, concat_axis=0, tiled=True)
    served = jnp.take(cache, asked.reshape(-1), axis=0).reshape(owners, cap, width)
    pulled = lax.all_to_all(
        served, ("blk", "img"), split_axis=0, concat_axis=0, tiled=True
    ).reshape(owners * cap, width)
    mate_emb = jnp.take(pulled, slot, axis=0).reshape(rows_dev, mates, width)
    mate_logit = (
        scale * jnp.einsum("rd,rkd->rk", images, mate_emb, preferred_element_type=jnp.float32)
        + offset
    )
    live = jnp.arange(mates, dtype=jnp.int32)[None, :] < mate_count[:, None]
    mate_coeff = jnp.where(live, scale * (jax.nn.sigmoid(mate_logit) - 1.0), 0.0).astype(
        jnp.bfloat16
    )
    slot_hits = slot[:, None] == jnp.arange(owners * cap, dtype=jnp.int32)[None, :]
    spread = jnp.where(slot_hits, mate_coeff.reshape(-1)[:, None].astype(jnp.float32), 0.0)
    weights = jnp.sum(spread.reshape(rows_dev, mates, owners * cap), axis=1).astype(jnp.bfloat16)
    image_grad = image_grad + jnp.dot(weights, pulled, preferred_element_type=jnp.float32)
    slot_grad = lax.dot_general(
        weights, images, (((0,), (0,)), ((), ())), preferred_element_type=jnp.float32
    )
    returned = lax.all_to_all(
        slot_grad.reshape(owners, cap, width),
        ("blk", "img"),
        split_axis=0,
        concat_axis=0,
        tiled=True,
    ).reshape(owners * cap, width)
    cache_rows = cache.shape[0]
    row_hits = (
        asked.reshape(-1)[:, None] == jnp.arange(cache_rows, dtype=jnp.int32)[None, :]
    ).astype(jnp.float32)
    cache_grad = lax.dot_general(
        row_hits,
        returned,
        (((0,), (0,)), ((), ())),
        precision=lax.Precision.HIGHEST,
        preferred_element_type=jnp.float32,
    )
    return (image_grad, text_grad, cache_grad)


def solution(mesh):
    return jax.shard_map(
        shards,
        mesh=mesh,
        in_specs=(
            P(("blk", "img"), None),
            P(("blk", "img"), None),
            P(("blk", "img"), None),
            P(("blk", "img"), None),
            P(("blk", "img"), None),
            P(("blk", "img")),
            P(),
            P(),
        ),
        out_specs=(P(("blk", "img"), None), P(("blk", "img"), None), P(("blk", "img"), None)),
        check_vma=False,
    )
```

profile of v0, /device:TPU:1, one launch (start us, length us, event | category | flops | bytes accessed | tf_op | source)
XLA Modules:
  0.0 421.3 jit_solution(16029337540523233288)
XLA Ops:
  7.2 0.0 copy-start
  7.2 0.0 all-gather.5.cloned.1.call-start
  7.2 0.7 all-gather.5.cloned.1.call-update
  7.9 0.0 all-gather.7.cloned.1.call-start
  8.0 0.7 all-gather.7.cloned.1.call-update
  8.7 0.0 all-gather.9.cloned.1.call-start
  8.7 0.7 all-gather.9.cloned.1.call-update
  9.4 0.0 all-gather.11.cloned.1.call-start
  9.4 0.5 all-gather.11.cloned.1.call-update
  10.0 0.8 copy.34
  10.8 0.1 eq.82
  10.9 0.1 eq.78
  11.0 0.7 broadcast_multiply_fusion
  11.7 0.1 copy.40
  11.8 0.1 mul.83
  11.9 0.1 copy.36
  12.0 0.2 fusion.26
  12.3 0.8 copy.41
  13.1 0.1 reshape.217
  13.2 0.2 fusion.24
  13.5 2.4 scatter_custom_fusion
  15.9 0.7 all_to_all.12
  16.6 11.5 %all-to-all-start = ((s32[128,1,8]{2,1,0:T(1,128)}), s32[128,1,8]{2,1,0:T(1,128)S(1)}, u32[]{:S(2)}, u32[]{:S(2)}) async-start(s32[128,1,8]{2,1,0:T(1,128)} %bitcast.7), calls=%async_computation.1 | async-start | bytes 131072 | tf_op jit(solution)/shard_map/all_to_all | solution.py:48
  29.5 8.3 %all-to-all-done = s32[128,1,8]{2,1,0:T(1,128)S(1)} async-done(((s32[128,1,8]{2,1,0:T(1,128)}), s32[128,1,8]{2,1,0:T(1,128)S(1)}, u32[]{:S(2)}, u32[]{:S(2)}) %all-to-all-start) | async-done | bytes 4128 | tf_op jit(solution)/shard_map/all_to_all | solution.py:48
  37.8 0.5 broadcast.212
  38.3 0.8 reduce.5
  39.2 0.1 reshape.192
  39.3 0.0 copy-done
  39.3 4.1 gather_fusion
  43.5 1.8 bitcast_select_fusion
  45.3 4.7 %all-to-all-start.1 = ((bf16[128,8,1152]{2,1,0:T(8,128)(2,1)}), bf16[128,8,1152]{2,1,0:T(8,128)(2,1)S(1)}, u32[]{:S(2)}, u32[]{:S(2)}) async-start(bf16[128,8,1152]{2,1,0:T(8,128)(2,1)} %bitcast_select_fusion), calls=%async_computation.2 | async-start | bytes 4718592 | tf_op jit(solution)/shard_map/all_to_all | solution.py:50
  49.9 0.2 reduce-scatter.3.cloned.1.call-start
  50.2 0.0 all-gather.5.cloned.1.call-done
  50.2 118.2 %all-gather.7.cloned.1.call-done = bf16[4096,1152]{1,0:T(8,128)(2,1)} async-done(((bf16[128,1152]{1,0:T(8,128)(2,1)}), bf16[4096,1152]{1,0:T(8,128)(2,1)}) %all-gather.7.cloned.1.call-update) | async-done | bytes 9437200 | tf_op jit(solution)/shard_map/all_gather | solution.py:31
  168.4 0.0 copy-start.2
  168.5 19.2 %fusion.5 = f32[512,1152]{1,0:T(8,128)} fusion(bf16[4096,1152]{1,0:T(8,128)(2,1)} %all-gather.7.cloned.1.call-done, bf16[512,1152]{1,0:T(8,128)(2,1)} %all-gather.5.cloned.1.call-done, s32[4096]{0:T(1024)S(1)} %fusion.40, f32[]{:T(128)} %bitcast.63, f32[]{:T(128)} %bitcast, s32[512]{0:T(512)S(1)} %iota_add_fusion), kind=kOutput, calls=%fused_computation.10 | convolution fusion | flops 9684647936 | bytes 12994568 | tf_op jit(solution)/shard_map/dot_general | solution.py:33
  187.6 0.0 reduce-scatter.3.cloned.1.call-update
  187.7 0.1 reduce_sum.23
  187.8 0.1 copy.38
  187.8 0.0 copy-done.2
  187.9 0.1 copy.39
  188.0 0.0 all-to-all-done.1
  188.0 0.0 copy-start.1
  188.0 3.1 gather_fusion.1
  191.1 0.0 copy-start.3
  191.1 3.2 gather.15
  194.4 0.0 copy-done.1
  194.4 3.4 fusion.18
  197.7 0.1 copy.44
  197.8 0.0 copy-done.3
  197.8 0.3 select_reduce_fusion
  198.2 2.9 convolution_bitcast_fusion
  201.1 7.0 %all-to-all-start.2 = ((f32[128,8,1152]{2,1,0:T(8,128)}), f32[128,8,1152]{2,1,0:T(8,128)}, u32[]{:S(2)}, u32[]{:S(2)}) async-start(f32[128,8,1152]{2,1,0:T(8,128)} %convolution_bitcast_fusion), calls=%async_computation.4 | async-start | bytes 9437184 | tf_op jit(solution)/shard_map/all_to_all | solution.py:69
  208.1 0.0 reduce-scatter.5.cloned.1.call-start
  208.2 0.0 all-gather.9.cloned.1.call-done
  208.2 140.8 %all-gather.11.cloned.1.call-done = bf16[4096,1152]{1,0:T(8,128)(2,1)} async-done(((bf16[128,1152]{1,0:T(8,128)(2,1)}), bf16[4096,1152]{1,0:T(8,128)(2,1)}) %all-gather.11.cloned.1.call-update) | async-done | bytes 9437200 | tf_op jit(solution)/shard_map/all_gather | solution.py:35
  349.0 19.3 %fusion.4 = f32[512,1152]{1,0:T(8,128)} fusion(bf16[4096,1152]{1,0:T(8,128)(2,1)} %all-gather.11.cloned.1.call-done, bf16[512,1152]{1,0:T(8,128)(2,1)} %all-gather.9.cloned.1.call-done, s32[4096]{0:T(1024)S(1)} %fusion.40, f32[]{:T(128)} %bitcast.65, f32[]{:T(128)} %bitcast, s32[512]{0:T(512)S(1)} %iota_add_fusion), kind=kOutput, calls=%fused_computation.9 | convolution fusion | flops 9684647936 | bytes 12994568 | tf_op jit(solution)/shard_map/dot_general | solution.py:37
  368.3 0.0 reduce-scatter.5.cloned.1.call-update
  368.3 0.1 reshape.194
  368.4 0.0 all-to-all-done.2
  368.4 5.2 %fusion.6 = f32[128,1152]{1,0:T(8,128)} fusion(f32[128,8,1152]{2,1,0:T(8,128)} %all-to-all-done.2, s32[1024]{0:T(1024)S(1)} %reshape.194), kind=kOutput, calls=%fused_computation.11 | convolution fusion | flops 1812070400 | bytes 5312512 | tf_op jit(solution)/shard_map/dot_general | solution.py:80
  373.6 6.7 %reduce-scatter.3.cloned.1.call-done = f32[128,1152]{1,0:T(8,128)} async-done(((f32[512,1152]{1,0:T(8,128)}), f32[128,1152]{1,0:T(8,128)}) %reduce-scatter.3.cloned.1.call-update) | async-done | bytes 589840 | tf_op jit(solution)/shard_map/reduce_scatter | solution.py:39
  380.3 2.4 convolution_add_fusion
  382.7 31.8 %reduce-scatter.5.cloned.1.call-done = f32[128,1152]{1,0:T(8,128)} async-done(((f32[512,1152]{1,0:T(8,128)}), f32[128,1152]{1,0:T(8,128)}) %reduce-scatter.5.cloned.1.call-update) | async-done | bytes 589840 | tf_op jit(solution)/shard_map/reduce_scatter | solution.py:38
  (15 shorter events, 0.2 us)
Async XLA Ops:
  7.2 32.1 %copy-start = (bf16[128,1152]{1,0:T(8,128)(2,1)S(1)}, bf16[128,1152]{1,0:T(8,128)(2,1)}, u32[]{:S(2)}) copy-start(bf16[128,1152]{1,0:T(8,128)(2,1)} %param.10) | copy-start | bytes 884740
  7.2 43.0 %all-gather.5.cloned.1.call-start = ((), (), s32[]{:S(2)}) async-start(), calls=%async_computation.5 | async-start | bytes 1474560 | tf_op jit(solution)/shard_map/all_gather | solution.py:18
  7.9 160.5 %all-gather.7.cloned.1.call-start = ((), (), s32[]{:S(2)}) async-start(), calls=%async_computation.6 | async-start | bytes 9732096 | tf_op jit(solution)/shard_map/all_gather | solution.py:31
  8.7 199.5 %all-gather.9.cloned.1.call-start = ((), (), s32[]{:S(2)}) async-start(), calls=%async_computation.8 | async-start | bytes 1474560 | tf_op jit(solution)/shard_map/all_gather | solution.py:34
  9.4 339.6 %all-gather.11.cloned.1.call-start = ((), (), s32[]{:S(2)}) async-start(), calls=%async_computation.9 | async-start | bytes 9732096 | tf_op jit(solution)/shard_map/all_gather | solution.py:35
  16.6 21.2 %all-to-all-start = ((s32[128,1,8]{2,1,0:T(1,128)}), s32[128,1,8]{2,1,0:T(1,128)S(1)}, u32[]{:S(2)}, u32[]{:S(2)}) async-start(s32[128,1,8]{2,1,0:T(1,128)} %bitcast.7), calls=%async_computation.1 | async-start | bytes 131072 | tf_op jit(solution)/shard_map/all_to_all | solution.py:48
  45.3 142.8 %all-to-all-start.1 = ((bf16[128,8,1152]{2,1,0:T(8,128)(2,1)}), bf16[128,8,1152]{2,1,0:T(8,128)(2,1)S(1)}, u32[]{:S(2)}, u32[]{:S(2)}) async-start(bf16[128,8,1152]{2,1,0:T(8,128)(2,1)} %bitcast_select_fusion), calls=%async_computation.2 | async-start | bytes 4718592 | tf_op jit(solution)/shard_map/all_to_all | solution.py:50
  49.9 330.3 %reduce-scatter.3.cloned.1.call-start = ((), (), s32[]{:S(2)}) async-start(), calls=%async_computation.7 | async-start | bytes 2949120 | tf_op jit(solution)/shard_map/reduce_scatter | solution.py:39
  168.4 19.4 %copy-start.2 = (s32[128,4]{0,1:T(4,128)S(1)}, s32[128,4]{0,1:T(4,128)}, u32[]{:S(2)}) copy-start(s32[128,4]{0,1:T(4,128)} %param.11) | copy-start | bytes 6148
  188.0 6.3 %copy-start.1 = (bf16[128,1152]{1,0:T(8,128)(2,1)S(1)}, bf16[128,1152]{1,0:T(8,128)(2,1)}, u32[]{:S(2)}) copy-start(bf16[128,1152]{1,0:T(8,128)(2,1)} %param.8) | copy-start | bytes 884740
  191.1 6.7 %copy-start.3 = (s32[128]{0:T(128)S(1)}, s32[128]{0:T(128)}, u32[]{:S(2)}) copy-start(s32[128]{0:T(128)} %param.13) | copy-start | bytes 1540
  201.1 167.3 %all-to-all-start.2 = ((f32[128,8,1152]{2,1,0:T(8,128)}), f32[128,8,1152]{2,1,0:T(8,128)}, u32[]{:S(2)}, u32[]{:S(2)}) async-start(f32[128,8,1152]{2,1,0:T(8,128)} %convolution_bitcast_fusion), calls=%async_computation.4 | async-start | bytes 9437184 | tf_op jit(solution)/shard_map/all_to_all | solution.py:69
  208.1 206.3 %reduce-scatter.5.cloned.1.call-start = ((), (), s32[]{:S(2)}) async-start(), calls=%async_computation.10 | async-start | bytes 2949120 | tf_op jit(solution)/shard_map/reduce_scatter | solution.py:38
Sparse Core Ops, SparseCore 0:
  9.7 26.0 all-gather.4
  38.8 129.6 all-gather.6
  170.1 20.3 all-gather.8
  193.3 155.6 all-gather.10
  351.3 28.9 reduce-scatter.2
  383.1 31.2 reduce-scatter.4
where the time goes:
time: 422 us; the launch traced here: 421 us
  waiting for transfers between devices  308 us (73%)
  matrix products  52.3 us (12%)
  starting transfers between devices  23.6 us (6%)
  local copies, waits for them, and re-layouts  17 us (4%)
  between operations  15.7 us (4%)
  other arithmetic  4.22 us (1%)
    all_gather x1, waiting for transfers between devices, shards(): piece = lax.all_gather(images, 'blk', axis=0, tiled=True)  141 us
    all_gather x1, waiting for transfers between devices, shards(): piece = lax.all_gather(texts, 'blk', axis=0, tiled=True)  118 us
    reduce_scatter x1, waiting for transfers between devices, shards(): lax.psum_scatter(partial_txt, 'img', scatter_dimension=0, tiled=True)  31.8 us
    dot_general x1, matrix products, shards(): partial_txt = jnp.dot(coeff, piece, preferred_element_type=jnp.float32)  19.3 us
    dot_general x1, matrix products, shards(): partial_img = jnp.dot(coeff, piece, preferred_element_type=jnp.float32)  19.2 us
    all_to_all x1, starting transfers between devices, shards(): lax.all_to_all(table, ('blk', 'img'), split_axis=0, concat_axis=0, tiled=...  11.5 us
  transfers between devices with their start and end apart: 9, of which 5 were waited for; matrix products, arithmetic and copies ran while one was open for 17% of the time, Pallas kernels for 0%

commit v1 on v0

v1 whole, which is shorter than its diff:
```python
import jax
import jax.numpy as jnp
from jax import lax
from jax.experimental import pallas as pl
from jax.experimental.pallas import tpu as pltpu
from jax.sharding import PartitionSpec as P

MESH = pl.DeviceIdType.MESH
F32, BF16, I32 = jnp.float32, jnp.bfloat16, jnp.int32
NT = (((1,), (1,)), ((), ()))
NN = (((1,), (0,)), ((), ()))
TN = (((0,), (0,)), ((), ()))
ROWS, D, HALF = 128, 1152, 64
LO, HI = pl.ds(0, HALF), pl.ds(HALF, HALF)


def mm(a, b, dims):
    return lax.dot_general(a, b, dims, preferred_element_type=F32)


def kernel(
    ls_ref, bias_ref, images, texts, cache, owner, row, count,
    ig_out, tg_out, cg_out,
    img, txt, cac, gat, tbl, coeff, tgrad, part, pbf, sgr,
    ra1, rb1, ra2, rb2, sa2, sb2, tsib, trec, csib, crec, tsx, trx, csx, crx,
    a_s, a_r, b_s, b_r, t_s, t_r, c_s, c_r, k_s, k_r,
    ra1_s, ra1_r, rb1_s, rb1_r, r2_s, r2_r, x_s, x_r,
):
    blk, im = lax.axis_index("blk"), lax.axis_index("img")
    z, y, x, c = blk // 8, (blk // 2) % 4, (blk % 2) * 2 + im // 2, im % 2

    def dev(dz=0, dy=0, dx=0, dc=0):
        zz, yy, xx = (z + dz + 4) % 4, (y + dy + 4) % 4, (x + dx + 4) % 4
        return ((zz * 4 + yy) * 2 + xx // 2, (xx % 2) * 2 + (c + dc) % 2)

    def rc(src, dst, ss, rs, to):
        return pltpu.make_async_remote_copy(
            src_ref=src, dst_ref=dst, send_sem=ss, recv_sem=rs, device_id=to, device_id_type=MESH
        )

    def img_a(dz, dy, d_z, d_y):
        return rc(img.at[dz * 4 + dy, LO], img.at[(dz + d_z) * 4 + dy + d_y, LO],
                  a_s.at[dz + d_z, dy + d_y], a_r.at[dz + d_z, dy + d_y], dev(-d_z, -d_y))

    def img_b(dz, dy, d_z, d_y):
        return rc(img.at[dz * 4 + dy, HI], img.at[(dz + d_z) * 4 + dy + d_y, HI],
                  b_s.at[dz + d_z, dy + d_y], b_r.at[dz + d_z, dy + d_y], dev(-d_z, -d_y))

    def got_a(dz, dy):
        rc(img.at[dz * 4 + dy, LO], img.at[dz * 4 + dy, LO], a_s.at[dz, dy], a_r.at[dz, dy], dev(0, 1)).wait_recv()

    def got_b(dz, dy):
        rc(img.at[dz * 4 + dy, HI], img.at[dz * 4 + dy, HI], b_s.at[dz, dy], b_r.at[dz, dy], dev(0, 1)).wait_recv()

    def rows_of(ref, n):
        return ref.at[pl.ds(n * ROWS, ROWS)]

    def along_x(ref, sems, semr, d):
        return rc(rows_of(ref, 0), rows_of(ref, 2 * d), sems.at[2 * d], semr.at[2 * d], dev(dx=-d))

    def to_sib(ref, sems, semr, d):
        return rc(rows_of(ref, 2 * d), rows_of(ref, 2 * d + 1), sems.at[2 * d + 1], semr.at[2 * d + 1], dev(dc=1))

    def tbl_y(d):
        return rc(tbl.at[0, 0], tbl.at[0, d], k_s.at[d], k_r.at[d], dev(0, -d))

    def tbl_z(d):
        return rc(tbl.at[0], tbl.at[d], k_s.at[3 + d], k_r.at[3 + d], dev(-d))

    peers = [dev(dy=d) for d in (1, 2, 3)] + [dev(dz=d) for d in (1, 2, 3)]
    peers += [dev(dx=d) for d in (1, 2, 3)] + [dev(dc=1)]
    barrier = pltpu.get_barrier_semaphore()
    for to in peers:
        pl.semaphore_signal(barrier, inc=1, device_id=to, device_id_type=MESH)
    img[0] = images[...]
    txt[0:ROWS] = texts[...]
    cac[0:ROWS] = cache[...]
    pl.semaphore_wait(barrier, len(peers))

    for d in (1, 3, 2):
        along_x(txt, t_s, t_r, d).start()
        img_a(0, 0, 0, d).start()
        img_b(0, 0, d, 0).start()
    to_sib(txt, t_s, t_r, 0).start()
    for d in (1, 3, 2):
        img_a(0, 0, d, 0).start()
        img_b(0, 0, 0, d).start()

    lane = lax.broadcasted_iota(I32, (ROWS, ROWS), 1)
    sub = lax.broadcasted_iota(I32, (ROWS, ROWS), 0)
    below = (sub > lane).astype(BF16)
    live = jnp.sum(jnp.where(sub == lane, count[...].astype(F32), 0.0), axis=1, keepdims=True)
    carry = jnp.zeros((1, ROWS), F32)
    picked_r = [jnp.zeros((1, ROWS), F32) for _ in range(8)]
    picked_c = [jnp.zeros((1, ROWS), F32) for _ in range(8)]
    row1 = (sub + 1).astype(F32)
    for k in range(4):
        hits = ((owner[:, k : k + 1] == lane) & (live > k)).astype(F32)
        rank = mm(below, hits.astype(BF16), NN) + carry
        carry = carry + jnp.sum(hits, axis=0, keepdims=True)
        cols = row[:, k : k + 1].astype(F32)
        for s in range(8):
            sel = jnp.where(rank == s, hits, 0.0)
            picked_r[s] = picked_r[s] + jnp.sum(sel * row1, axis=0, keepdims=True)
            picked_c[s] = picked_c[s] + jnp.sum(sel * cols, axis=0, keepdims=True)
    for s in range(8):
        tbl[0, 0, s : s + 1, :] = picked_r[s].astype(I32)
        tbl[0, 0, 8 + s : 9 + s, :] = picked_c[s].astype(I32)
    for d in (1, 3, 2):
        tbl_y(d).start()

    for d in (1, 3, 2):
        got_a(0, d)
        for e in (1, 3, 2):
            img_a(0, d, e, 0).start()
        got_b(d, 0)
        for e in (1, 3, 2):
            img_b(d, 0, 0, e).start()
        tbl_y(d).wait_recv()
    for d in (1, 3, 2):
        tbl_z(d).start()
    tgrad[...] = jnp.zeros_like(tgrad)
    for d in (1, 3, 2):
        along_x(txt, t_s, t_r, d).wait_recv()
        to_sib(txt, t_s, t_r, d).start()
        along_x(cac, c_s, c_r, d).start()
    to_sib(cac, c_s, c_r, 0).start()
    for d in range(4):
        to_sib(txt, t_s, t_r, d).wait_recv()
    for d in (1, 2, 3):
        tbl_z(d).wait_recv()

    scale = jnp.exp(ls_ref[...])
    half = 0.5 * scale
    shift = 0.5 * bias_ref[...]

    def place(i):
        q, p = i // 2, i % 2
        return q + q // 2 - 2 * (q // 3), p

    def text_step(i):
        dz, p = place(i)
        for j in (0, 1):
            dy = 2 * p + j

            @pl.when(dz != 0)
            def _():
                got_a(dz, dy)

            @pl.when(dy != 0)
            def _():
                got_b(dz, dy)

        pair = dz * 2 + p
        mine = img[pl.ds(pair * 2, 2)].reshape(2 * ROWS, D)
        logit = mm(mine, txt[...], NT)
        coeff[...] = (half + half * jnp.tanh(half * logit + shift)).astype(BF16)

        @pl.when(i == 0)
        def _():
            own = mm(img[0], txt[0:ROWS], NT)
            prob = half + half * jnp.tanh(half * own + shift)
            coeff[0:ROWS, 0:ROWS] = (prob - jnp.where(sub == lane, scale, 0.0)).astype(BF16)

        co = coeff[...]
        part[pl.ds(pair * 2, 2)] = mm(co, txt[...], NN).reshape(2, ROWS, D)
        tgrad[...] += mm(co, mine, TN)

    def spread_lanes(table, first):
        want = lax.broadcasted_iota(I32, (ROWS, ROWS), 0)
        b = lax.broadcasted_iota(I32, (ROWS, ROWS), 1) // 16
        of = first + ((x + b // 2) % 4) * 2 + (c + b) % 2
        return mm(table, (want == of).astype(BF16), NN)

    first = (z * 4 + y) * 8
    tab = tbl[...].reshape(16, 2, 8, ROWS)
    tab_r = tab[:, 0].reshape(ROWS, ROWS).astype(F32).astype(BF16)
    tab_c = tab[:, 1].reshape(ROWS, ROWS).astype(F32).astype(BF16)

    def column(b):
        of = first + ((x + b // 2) % 4) * 2 + (c + b) % 2
        want = lax.broadcasted_iota(I32, (ROWS, ROWS), 0)
        return (mm(tab_c, (want == of).astype(BF16), NN) == lane.astype(F32)).astype(BF16)

    lanes_r = spread_lanes(tab_r, first)

    def gather_rows():
        for d in (1, 3, 2):
            along_x(cac, c_s, c_r, d).wait_recv()
            to_sib(cac, c_s, c_r, d).start()
        for d in range(4):
            to_sib(cac, c_s, c_r, d).wait_recv()
        for b in range(8):
            gat[b] = mm(column(b), cac[pl.ds(b * ROWS, ROWS)], NN).astype(BF16)

    def a1(dz, dy):
        return rc(pbf.at[dz * 4 + dy, LO], ra1.at[dz, dy], ra1_s.at[dz, dy], ra1_r.at[dz, dy], dev(dz))

    def b1(dz, dy):
        return rc(pbf.at[dz * 4 + dy, HI], rb1.at[dy, dz], rb1_s.at[dz, dy], rb1_r.at[dz, dy], dev(0, dy))

    def mate_step(i):
        dz, p = place(i)
        pair = dz * 2 + p
        mine = img[pl.ds(pair * 2, 2)].reshape(2 * ROWS, D)
        emb = gat[:, pl.ds(pair * 16, 16), :].reshape(ROWS, D)
        keep = jnp.where(sub == pair * 16 + lane % 16, lanes_r, 0.0)
        at_row = jnp.sum(keep, axis=0, keepdims=True)
        big_sub = lax.broadcasted_iota(I32, (2 * ROWS, ROWS), 0)
        second = lax.broadcasted_iota(I32, (1, ROWS), 1) % 16 // 8
        target = jnp.where(at_row > 0.5, at_row - 1.0 + second.astype(F32) * ROWS, -1.0)
        named = big_sub.astype(F32) == target
        logit = mm(mine, emb, NT)
        wt = jnp.where(named, half * jnp.tanh(half * logit + shift) - half, 0.0).astype(BF16)
        total = part[pl.ds(pair * 2, 2)].reshape(2 * ROWS, D) + mm(wt, emb, NN)
        part[pl.ds(pair * 2, 2)] = total.reshape(2, ROWS, D)
        pbf[pl.ds(pair * 2, 2)] = total.astype(BF16).reshape(2, ROWS, D)
        slots = mm(wt, mine, TN)
        top = slots.astype(BF16)
        sgr[:, 0, pl.ds(pair * 16, 16), :] = top.reshape(8, 16, D)
        sgr[:, 1, pl.ds(pair * 16, 16), :] = (slots - top.astype(F32)).astype(BF16).reshape(8, 16, D)
        for j in (0, 1):
            dy = 2 * p + j

            @pl.when(dz != 0)
            def _():
                a1(dz, dy).start()

            @pl.when(dy != 0)
            def _():
                b1(dz, dy).start()

    lag = 3

    def step(i, carried):
        @pl.when(i < 8)
        def _():
            text_step(i)

        @pl.when(i == lag)
        def _():
            gather_rows()

        @pl.when(i >= lag)
        def _():
            mate_step(i - lag)

        return carried

    lax.fori_loop(0, 8 + lag, step, 0)

    def sib(buf, rec, base, d):
        return rc(buf.at[d], rec.at[d], x_s.at[base + d], x_r.at[base + d], dev(dc=1))

    def xs(buf, rec, base, d):
        return rc(buf.at[d], rec.at[d], x_s.at[base + d], x_r.at[base + d], dev(dx=d))

    for d in (2, 1, 3, 0):
        tsib[d] = tgrad[pl.ds((2 * d + 1) * ROWS, ROWS)].astype(BF16)
        sib(tsib, trec, 0, d).start()

    def owner_grad(b):
        spots = column(b)
        both = jnp.concatenate([spots, spots], axis=0)
        return mm(both, sgr[b].reshape(2 * ROWS, D), TN)

    for d in (2, 1, 3, 0):
        csib[d] = owner_grad(2 * d + 1).astype(BF16)
        sib(csib, crec, 4, d).start()
    for d in (2, 1, 3):
        sib(tsib, trec, 0, d).wait_recv()
        tsx[d] = (tgrad[pl.ds(2 * d * ROWS, ROWS)] + trec[d].astype(F32)).astype(BF16)
        xs(tsx, trx, 8, d).start()
    for d in (2, 1, 3):
        own = owner_grad(2 * d)
        sib(csib, crec, 4, d).wait_recv()
        csx[d] = (own + crec[d].astype(F32)).astype(BF16)
        xs(csx, crx, 12, d).start()

    def a2(d):
        return rc(sa2.at[d], ra2.at[d], r2_s.at[d], r2_r.at[d], dev(0, d))

    def b2(d):
        return rc(sb2.at[d], rb2.at[d], r2_s.at[4 + d], r2_r.at[4 + d], dev(d))

    for d in (2, 1, 3, 0):
        for e in (1, 2, 3):
            a1(e, d).wait_recv()
            b1(d, e).wait_recv()
        sum_a = part[d, 0:HALF] + ra1[1, d].astype(F32) + ra1[2, d].astype(F32) + ra1[3, d].astype(F32)
        sum_b = part[4 * d, HALF:] + rb1[1, d].astype(F32) + rb1[2, d].astype(F32) + rb1[3, d].astype(F32)
        if d:
            sa2[d] = sum_a.astype(BF16)
            a2(d).start()
            sb2[d] = sum_b.astype(BF16)
            b2(d).start()
        else:
            part[0, 0:HALF] = sum_a
            part[0, HALF:] = sum_b

    sib(tsib, trec, 0, 0).wait_recv()
    for d in (1, 2, 3):
        xs(tsx, trx, 8, d).wait_recv()
    tg_out[...] = (tgrad[0:ROWS] + trec[0].astype(F32) + trx[1].astype(F32) + trx[2].astype(F32) + trx[3].astype(F32))
    own = owner_grad(0)
    sib(csib, crec, 4, 0).wait_recv()
    for d in (1, 2, 3):
        xs(csx, crx, 12, d).wait_recv()
    cg_out[...] = own + crec[0].astype(F32) + crx[1].astype(F32) + crx[2].astype(F32) + crx[3].astype(F32)
    for d in (1, 2, 3):
        a2(d).wait_recv()
        b2(d).wait_recv()
    ig_out[0:HALF] = part[0, 0:HALF] + ra2[1].astype(F32) + ra2[2].astype(F32) + ra2[3].astype(F32)
    ig_out[HALF:] = part[0, HALF:] + rb2[1].astype(F32) + rb2[2].astype(F32) + rb2[3].astype(F32)

    for d in (1, 2, 3):
        for e in range(4):
            img_a(0, e, d, 0).wait_send()
            img_b(e, 0, 0, d).wait_send()
            a1(d, e).wait_send()
            b1(e, d).wait_send()
        img_a(0, 0, 0, d).wait_send()
        img_b(0, 0, d, 0).wait_send()
        for ref, ss, sr in ((txt, t_s, t_r), (cac, c_s, c_r)):
            along_x(ref, ss, sr, d).wait_send()
        tbl_y(d).wait_send()
        tbl_z(d).wait_send()
        xs(tsx, trx, 8, d).wait_send()
        xs(csx, crx, 12, d).wait_send()
        a2(d).wait_send()
        b2(d).wait_send()
    for d in range(4):
        to_sib(txt, t_s, t_r, d).wait_send()
        to_sib(cac, c_s, c_r, d).wait_send()
        sib(tsib, trec, 0, d).wait_send()
        sib(csib, crec, 4, d).wait_send()


def shards(images, texts, cache, mate_owner, mate_row, mate_count, log_scale, bias):
    vm = pl.BlockSpec(memory_space=pltpu.VMEM)
    dma = pltpu.SemaphoreType.DMA
    out = jax.ShapeDtypeStruct((ROWS, D), F32)
    four = lambda rows: pltpu.VMEM((4, rows, D), BF16)
    return tuple(
        pl.pallas_call(
            kernel,
            out_shape=(out, out, out),
            in_specs=[vm] * 8,
            out_specs=(vm, vm, vm),
            scratch_shapes=[
                pltpu.VMEM((16, ROWS, D), BF16),
                pltpu.VMEM((8 * ROWS, D), BF16),
                pltpu.VMEM((8 * ROWS, D), BF16),
                pltpu.VMEM((8, ROWS, D), BF16),
                pltpu.VMEM((4, 4, 16, ROWS), I32),
                pltpu.VMEM((2 * ROWS, 8 * ROWS), BF16),
                pltpu.VMEM((8 * ROWS, D), F32),
                pltpu.VMEM((16, ROWS, D), F32),
                pltpu.VMEM((16, ROWS, D), BF16),
                pltpu.VMEM((8, 2, ROWS, D), BF16),
                pltpu.VMEM((4, 4, HALF, D), BF16),
                pltpu.VMEM((4, 4, HALF, D), BF16),
                four(HALF), four(HALF), four(HALF), four(HALF),
                four(ROWS), four(ROWS), four(ROWS), four(ROWS),
                four(ROWS), four(ROWS), four(ROWS), four(ROWS),
                dma((4, 4)), dma((4, 4)), dma((4, 4)), dma((4, 4)),
                dma((8,)), dma((8,)), dma((8,)), dma((8,)),
                dma((8,)), dma((8,)),
                dma((4, 4)), dma((4, 4)), dma((4, 4)), dma((4, 4)),
                dma((8,)), dma((8,)), dma((16,)), dma((16,)),
            ],
            compiler_params=pltpu.CompilerParams(
                collective_id=0, has_side_effects=True, vmem_limit_bytes=62 << 20
            ),
            cost_estimate=pl.CostEstimate(flops=17_000_000_000, bytes_accessed=4_000_000, transcendentals=2_000_000),
        )(
            log_scale.reshape(1, 1), bias.reshape(1, 1), images, texts, cache,
            mate_owner, mate_row, mate_count.reshape(1, ROWS),
        )
    )


def solution(mesh):
    rows = P(("blk", "img"), None)
    return jax.shard_map(
        shards,
        mesh=mesh,
        in_specs=(rows, rows, rows, rows, rows, P(("blk", "img")), P(), P()),
        out_specs=(rows, rows, rows),
        check_vma=False,
    )
```

time: 422 us -> 117 us (0.28)
  waiting for transfers between devices: 308 us -> 0 us
  Pallas kernels: 0 us -> 108 us
  matrix products: 52.3 us -> 0 us
  starting transfers between devices: 23.6 us -> 0 us
  between operations: 15.7 us -> 1.95 us
  local copies, waits for them, and re-layouts: 17 us -> 6.23 us
  other arithmetic: 4.22 us -> 0 us
    all_gather x4 -> x0, waiting for transfers between devices: 259 us -> none  [the longest x1 141 us: shards(): piece = lax.all_gather(images, 'blk', axis=0, tiled=True)]
    pallas_call x0 -> x1, Pallas kernels: none -> 108 us  [shards(): pl.pallas_call(kernel, out_shape=(out, out, out), in_specs=[vm] * 8, out_...]
    dot_general x6 -> x0, matrix products: 52.3 us -> none  [the longest x1 19.3 us: shards(): partial_txt = jnp.dot(coeff, piece, preferred_element_type=jnp.float32)]
    reduce_scatter x2 -> x0, waiting for transfers between devices: 38.5 us -> none  [the longest x1 31.8 us: shards(): lax.psum_scatter(partial_txt, 'img', scatter_dimension=0, tiled=True)]
    all_to_all x3 -> x0, starting transfers between devices: 23.2 us -> none  [the longest x1 11.5 us: shards(): lax.all_to_all(table, ('blk', 'img'), split_axis=0, concat_axis=0, tiled=...]
    gather x3 -> x0, local copies, waits for them, and re-layouts: 10.5 us -> none  [the longest x2 6.32 us: shards(): mate_emb = jnp.take(pulled, slot, axis=0).reshape(rows_dev, mates, width)]
    all_to_all x3 -> x0, waiting for transfers between devices: 8.32 us -> none  [the longest x1 8.31 us: shards(): lax.all_to_all(table, ('blk', 'img'), split_axis=0, concat_axis=0, tiled=...]
    unnamed x11 -> x13, local copies, waits for them, and re-layouts: 1.61 us -> 6.23 us
  transfers between devices with their start and end apart: 9 -> 0, of which waited for: 5 -> 0; matrix products, arithmetic and copies ran while one was open for 17% -> 0% of each run, Pallas kernels for 0% -> 0%
where the time goes in v1:
time: 117 us
  Pallas kernels  108 us (92%)
  local copies, waits for them, and re-layouts  6.23 us (5%)
  between operations  1.95 us (2%)
    pallas_call x1, Pallas kernels, shards(): pl.pallas_call(kernel, out_shape=(out, out, out), in_specs=[vm] * 8, out_...  108 us
    unnamed x13, local copies, waits for them, and re-layouts  6.23 us

profile of v1, /device:TPU:1, one launch (start us, length us, event | category | flops | bytes accessed | tf_op | source)
XLA Modules:
  0.0 116.7 jit_solution(10755988860027414318)
XLA Ops:
  1.9 0.0 copy-start.2
  1.9 0.7 copy-done.2
  2.6 0.0 copy-start.3
  2.6 0.7 copy.11.owner
  3.3 0.0 copy-done.3
  3.4 0.7 copy.12.row
  4.1 108.5 %shard_map.103 = (f32[128,1152]{1,0:T(8,128)}, f32[128,1152]{1,0:T(8,128)}, f32[128,1152]{1,0:T(8,128)}) custom-call(f32[1,1]{1,0:T(1,128)} %bitcast.3.ls_ref, f32[1,1]{1,0:T(1,128)} %bitcast.4.bias_ref, bf16[128,1152]{1,0:T(8,128)(2,1)} %images.1, bf16[128,1152]{1,0:T(8,128)(2,1)} %texts.1, bf16[128,1152]{1,0:T(8,128)(2,1)} %cache.1, s32[128,4]{1,0:T(8,128)} %copy.11.owner, ...), custom_call_target="tpu_custom_call" | custom-call | flops 16999999488 | bytes 4000000 | tf_op jit(solution)/shard_map/pallas_call | solution.py:345
  112.6 0.0 copy-start.1
  112.6 2.0 %copy.18 = f32[128,1152]{1,0:T(8,128)} copy(f32[128,1152]{1,0:T(8,128)} %get-tuple-element.6) | data formatting | bytes 1179648
  114.6 0.0 copy-done.1
  114.6 0.0 copy-start
  114.6 0.8 copy.19
  115.4 0.5 copy-done
  115.9 0.8 copy.20
Async XLA Ops:
  1.9 0.7 copy-start.2
  2.6 0.7 copy-start.3
  112.6 2.0 %copy-start.1 = (f32[128,1152]{1,0:T(8,128)S(1)}, f32[128,1152]{1,0:T(8,128)}, u32[]{:S(2)}) copy-start(f32[128,1152]{1,0:T(8,128)} %get-tuple-element.7) | copy-start | bytes 1769476
  114.6 1.3 %copy-start = (f32[128,1152]{1,0:T(8,128)S(1)}, f32[128,1152]{1,0:T(8,128)}, u32[]{:S(2)}) copy-start(f32[128,1152]{1,0:T(8,128)} %get-tuple-element.8) | copy-start | bytes 1769476

commit v2 on v1

v2 whole, which is shorter than its diff:
```python
import jax
import jax.numpy as jnp
from jax import lax
from jax.experimental import pallas as pl
from jax.experimental.pallas import tpu as pltpu
from jax.sharding import PartitionSpec as P

MESH = pl.DeviceIdType.MESH
F32, BF16, I32 = jnp.float32, jnp.bfloat16, jnp.int32
NT = (((1,), (1,)), ((), ()))
NN = (((1,), (0,)), ((), ()))
TN = (((0,), (0,)), ((), ()))
ROWS, D, HALF, QTR = 128, 1152, 64, 32
LO, HI = pl.ds(0, HALF), pl.ds(HALF, HALF)
QUARTERS = tuple(pl.ds(q * QTR, QTR) for q in range(4))


def mm(a, b, dims):
    return lax.dot_general(a, b, dims, preferred_element_type=F32)


def kernel(
    ls_ref, bias_ref, images, texts, cache, owner, row, count,
    ig_out, tg_out, cg_out,
    img, txt, cac, gat, tbl, coeff, tgrad, part, pbf, sgr,
    rqa, rqb, rha, rhb, usend, uq, uh, tsib, trec, csib, crec, tsx, trx, csx, crx,
    a_s, a_r, b_s, b_r, aq_s, aq_r, bq_s, bq_r, t_s, t_r, c_s, c_r, k_s, k_r,
    rqa_s, rqa_r, rqb_s, rqb_r, rha_s, rha_r, rhb_s, rhb_r, u_s, u_r, x_s, x_r,
):
    blk, im = lax.axis_index("blk"), lax.axis_index("img")
    z, y, x, c = blk // 8, (blk // 2) % 4, (blk % 2) * 2 + im // 2, im % 2

    def dev(dz=0, dy=0, dx=0, dc=0):
        zz, yy, xx = (z + dz + 4) % 4, (y + dy + 4) % 4, (x + dx + 4) % 4
        return ((zz * 4 + yy) * 2 + xx // 2, (xx % 2) * 2 + (c + dc) % 2)

    def rc(src, dst, ss, rs, to):
        return pltpu.make_async_remote_copy(
            src_ref=src, dst_ref=dst, send_sem=ss, recv_sem=rs, device_id=to, device_id_type=MESH
        )

    def blk_a(n):
        return img.at[n, LO]

    def blk_b(n):
        return img.at[n, HI]

    def a_y(d):
        return rc(blk_a(0), blk_a(d), a_s.at[0, d], a_r.at[0, d], dev(0, -d))

    def b_z(d):
        return rc(blk_b(0), blk_b(4 * d), b_s.at[d, 0], b_r.at[d, 0], dev(-d))

    def a_z(dy, d):
        return rc(blk_a(dy), blk_a(4 * d + dy), a_s.at[d, dy], a_r.at[d, dy], dev(-d))

    def b_y(dz, d):
        return rc(blk_b(4 * dz), blk_b(4 * dz + d), b_s.at[dz, d], b_r.at[dz, d], dev(0, -d))

    def aq_y(d):
        q = QUARTERS[d // 2]
        return rc(img.at[d, q], img.at[2, q], aq_s.at[d // 2, 4], aq_r.at[d // 2, 4], dev(0, -d))

    def bq_z(d):
        q = QUARTERS[2 + d // 2]
        return rc(img.at[4 * d, q], img.at[8, q], bq_s.at[d // 2, 4], bq_r.at[d // 2, 4], dev(-d))

    def aq_z(dy, d):
        q = QUARTERS[d // 2]
        return rc(img.at[4 * d + dy, q], img.at[8 + dy, q], aq_s.at[d // 2, dy], aq_r.at[d // 2, dy], dev(-d))

    def bq_y(dz, d):
        q = QUARTERS[2 + d // 2]
        return rc(img.at[4 * dz + d, q], img.at[4 * dz + 2, q], bq_s.at[d // 2, dz], bq_r.at[d // 2, dz], dev(0, -d))

    def rows_of(ref, n):
        return ref.at[pl.ds(n * ROWS, ROWS)]

    def along_x(ref, sems, semr, d):
        return rc(rows_of(ref, 0), rows_of(ref, 2 * d), sems.at[2 * d], semr.at[2 * d], dev(dx=-d))

    def half_x(ref, sems, semr, d):
        h = d // 2 * HALF
        return rc(ref.at[pl.ds(2 * d * ROWS + h, HALF)], ref.at[pl.ds(4 * ROWS + h, HALF)],
                  sems.at[8 + d], semr.at[8 + d], dev(dx=-d))

    def to_sib(ref, sems, semr, d):
        return rc(rows_of(ref, 2 * d), rows_of(ref, 2 * d + 1), sems.at[2 * d + 1], semr.at[2 * d + 1], dev(dc=1))

    def tbl_y(d):
        return rc(tbl.at[0, 0], tbl.at[0, d], k_s.at[d], k_r.at[d], dev(0, -d))

    def tbl_y2():
        return rc(tbl.at[0, 1], tbl.at[0, 2], k_s.at[2], k_r.at[2], dev(0, -1))

    def tbl_z(d):
        return rc(tbl.at[0], tbl.at[d], k_s.at[4 + d], k_r.at[4 + d], dev(-d))

    def tbl_z2():
        return rc(tbl.at[1], tbl.at[2], k_s.at[6], k_r.at[6], dev(-1))

    peers = [dev(dy=1), dev(dy=3), dev(dz=1), dev(dz=3), dev(dx=1), dev(dx=3), dev(dc=1)]
    barrier = pltpu.get_barrier_semaphore()
    for to in peers:
        pl.semaphore_signal(barrier, inc=1, device_id=to, device_id_type=MESH)
    img[0] = images[...]
    txt[0:ROWS] = texts[...]
    cac[0:ROWS] = cache[...]
    pl.semaphore_wait(barrier, len(peers))

    for d in (1, 3):
        a_y(d).start()
        b_z(d).start()
        along_x(txt, t_s, t_r, d).start()
    to_sib(txt, t_s, t_r, 0).start()
    for d in (1, 3):
        b_y(0, d).start()
        a_z(0, d).start()

    lane = lax.broadcasted_iota(I32, (ROWS, ROWS), 1)
    sub = lax.broadcasted_iota(I32, (ROWS, ROWS), 0)
    below = (sub > lane).astype(BF16)

    def down(line):
        return jnp.transpose(jnp.broadcast_to(line.astype(F32), (ROWS, ROWS)))

    live = down(count[...])
    carry = jnp.zeros((1, ROWS), F32)
    picked_r = [jnp.zeros((1, ROWS), F32) for _ in range(8)]
    picked_c = [jnp.zeros((1, ROWS), F32) for _ in range(8)]
    row1 = (sub + 1).astype(F32)
    for k in range(4):
        hits = ((down(owner[k : k + 1, :]) == lane.astype(F32)) & (live > k)).astype(F32)
        rank = mm(below, hits.astype(BF16), NN) + carry
        carry = carry + jnp.sum(hits, axis=0, keepdims=True)
        cols = down(row[k : k + 1, :])
        for s in range(8):
            sel = jnp.where(rank == s, hits, 0.0)
            picked_r[s] = picked_r[s] + jnp.sum(sel * row1, axis=0, keepdims=True)
            picked_c[s] = picked_c[s] + jnp.sum(sel * cols, axis=0, keepdims=True)
    for s in range(8):
        tbl[0, 0, s : s + 1, :] = picked_r[s].astype(I32)
        tbl[0, 0, 8 + s : 9 + s, :] = picked_c[s].astype(I32)
    for d in (1, 3):
        tbl_y(d).start()

    for d in (1, 3):
        a_y(d).wait_recv()
        aq_y(d).start()
        for e in (1, 3):
            a_z(d, e).start()
        b_z(d).wait_recv()
        bq_z(d).start()
        for e in (1, 3):
            b_y(d, e).start()
    for d in (1, 3):
        tbl_y(d).wait_recv()
        if d == 1:
            tbl_y2().start()
    for d in (1, 3):
        b_y(0, d).wait_recv()
        bq_y(0, d).start()
        a_z(0, d).wait_recv()
        aq_z(0, d).start()
    tbl_y2().wait_recv()
    for d in (1, 3):
        tbl_z(d).start()
    tgrad[...] = jnp.zeros_like(tgrad)
    for d in (1, 3):
        along_x(txt, t_s, t_r, d).wait_recv()
        half_x(txt, t_s, t_r, d).start()
        to_sib(txt, t_s, t_r, d).start()
    for d in (1, 3):
        along_x(cac, c_s, c_r, d).start()
    to_sib(cac, c_s, c_r, 0).start()
    for d in (1, 3):
        aq_y(d).wait_recv()
        bq_z(d).wait_recv()
    for d in (1, 3):
        a_z(2, d).start()
        b_y(2, d).start()
    for d in (1, 3):
        tbl_z(d).wait_recv()
        if d == 1:
            tbl_z2().start()
    for d in (1, 3):
        half_x(txt, t_s, t_r, d).wait_recv()
    to_sib(txt, t_s, t_r, 2).start()

    def corners():
        for e in (1, 3):
            for d in (1, 3):
                a_z(e, d).wait_recv()
                aq_z(e, d).start()
                b_y(e, d).wait_recv()
                bq_y(e, d).start()

    def edges():
        for d in (1, 3):
            a_z(2, d).wait_recv()
            aq_z(2, d).start()
            b_y(2, d).wait_recv()
            bq_y(2, d).start()

    def cache_near():
        for d in (1, 3):
            along_x(cac, c_s, c_r, d).wait_recv()
            half_x(cac, c_s, c_r, d).start()
            to_sib(cac, c_s, c_r, d).start()

    def cache_far():
        for d in (1, 3):
            half_x(cac, c_s, c_r, d).wait_recv()
        to_sib(cac, c_s, c_r, 2).start()

    def last_dz0():
        for d in (1, 3):
            bq_y(0, d).wait_recv()

    def last_dz(e):
        for d in (1, 3):
            bq_y(e, d).wait_recv()

    def last_quarters():
        for e in range(4):
            for d in (1, 3):
                aq_z(e, d).wait_recv()
        last_dz(2)

    for d in range(4):
        to_sib(txt, t_s, t_r, d).wait_recv()
    tbl_z2().wait_recv()

    scale = jnp.exp(ls_ref[...])
    half = 0.5 * scale
    shift = 0.5 * bias_ref[...]

    def place(i):
        q, p = i // 2, i % 2
        return q + q // 2 - 2 * (q // 3), p

    def text_step(i):
        dz, p = place(i)
        pair = dz * 2 + p
        mine = img[pl.ds(pair * 2, 2)].reshape(2 * ROWS, D)
        logit = mm(mine, txt[...], NT)
        coeff[...] = (half + half * jnp.tanh(half * logit + shift)).astype(BF16)

        @pl.when(i == 0)
        def _():
            own = mm(img[0], txt[0:ROWS], NT)
            prob = half + half * jnp.tanh(half * own + shift)
            coeff[0:ROWS, 0:ROWS] = (prob - jnp.where(sub == lane, scale, 0.0)).astype(BF16)

        co = coeff[...]
        part[pl.ds(pair * 2, 2)] = mm(co, txt[...], NN).reshape(2, ROWS, D)
        tgrad[...] += mm(co, mine, TN)

    def spread_lanes(table, first):
        want = lax.broadcasted_iota(I32, (ROWS, ROWS), 0)
        b = lax.broadcasted_iota(I32, (ROWS, ROWS), 1) // 16
        of = first + ((x + b // 2) % 4) * 2 + (c + b) % 2
        return mm(table, (want == of).astype(BF16), NN)

    first = (z * 4 + y) * 8
    tab = tbl[...].reshape(16, 2, 8, ROWS)
    tab_r = tab[:, 0].reshape(ROWS, ROWS).astype(F32).astype(BF16)
    tab_c = tab[:, 1].reshape(ROWS, ROWS).astype(F32).astype(BF16)

    def column(b):
        of = first + ((x + b // 2) % 4) * 2 + (c + b) % 2
        want = lax.broadcasted_iota(I32, (ROWS, ROWS), 0)
        return (mm(tab_c, (want == of).astype(BF16), NN) == lane.astype(F32)).astype(BF16)

    lanes_r = spread_lanes(tab_r, first)

    def gather_rows():
        for d in range(4):
            to_sib(cac, c_s, c_r, d).wait_recv()
        for b in range(8):
            gat[b] = mm(column(b), cac[pl.ds(b * ROWS, ROWS)], NN).astype(BF16)

    def far_a(dy, d):
        q = QUARTERS[d // 2]
        return rc(pbf.at[8 + dy, q], rqa.at[d // 2, dy], rqa_s.at[d // 2, dy], rqa_r.at[d // 2, dy], dev(d))

    def far_b(dz, d):
        q = QUARTERS[2 + d // 2]
        return rc(pbf.at[4 * dz + 2, q], rqb.at[d // 2, dz], rqb_s.at[d // 2, dz], rqb_r.at[d // 2, dz], dev(0, d))

    def near_a(dy, d):
        return rc(pbf.at[4 * d + dy, LO], rha.at[d // 2, dy], rha_s.at[d // 2, dy], rha_r.at[d // 2, dy], dev(d))

    def near_b(dz, d):
        return rc(pbf.at[4 * dz + d, HI], rhb.at[d // 2, dz], rhb_s.at[d // 2, dz], rhb_r.at[d // 2, dz], dev(0, d))

    def mate_step(i):
        dz, p = place(i)
        pair = dz * 2 + p
        mine = img[pl.ds(pair * 2, 2)].reshape(2 * ROWS, D)
        emb = gat[:, pl.ds(pair * 16, 16), :].reshape(ROWS, D)
        keep = jnp.where(sub == pair * 16 + lane % 16, lanes_r, 0.0)
        at_row = jnp.sum(keep, axis=0, keepdims=True)
        big_sub = lax.broadcasted_iota(I32, (2 * ROWS, ROWS), 0)
        second = lax.broadcasted_iota(I32, (1, ROWS), 1) % 16 // 8
        target = jnp.where(at_row > 0.5, at_row - 1.0 + second.astype(F32) * ROWS, -1.0)
        named = big_sub.astype(F32) == target
        logit = mm(mine, emb, NT)
        wt = jnp.where(named, half * jnp.tanh(half * logit + shift) - half, 0.0).astype(BF16)
        total = part[pl.ds(pair * 2, 2)].reshape(2 * ROWS, D) + mm(wt, emb, NN)
        part[pl.ds(pair * 2, 2)] = total.reshape(2, ROWS, D)
        pbf[pl.ds(pair * 2, 2)] = total.astype(BF16).reshape(2, ROWS, D)
        slots = mm(wt, mine, TN)
        top = slots.astype(BF16)
        sgr[:, 0, pl.ds(pair * 16, 16), :] = top.reshape(8, 16, D)
        sgr[:, 1, pl.ds(pair * 16, 16), :] = (slots - top.astype(F32)).astype(BF16).reshape(8, 16, D)
        for d in (1, 3):
            @pl.when(dz == 2)
            def _():
                far_a(2 * p, d).start()
                far_a(2 * p + 1, d).start()

            @pl.when(p == 1)
            def _():
                far_b(dz, d).start()

    lag = 4

    def step(i, carried):
        @pl.when(i == 2)
        def _():
            corners()

        @pl.when(i == 1)
        def _():
            last_dz0()

        @pl.when(i == 3)
        def _():
            edges()
            cache_near()
            last_dz(1)

        @pl.when(i == 4)
        def _():
            last_dz(3)

        @pl.when(i == 6)
        def _():
            last_quarters()

        @pl.when(i < 8)
        def _():
            text_step(i)

        @pl.when(i == lag)
        def _():
            cache_far()
            gather_rows()

        @pl.when(i >= lag)
        def _():
            mate_step(i - lag)

        return carried

    lax.fori_loop(0, 8 + lag, step, 0)

    def near_sends(e):
        for d in (1, 3):
            far_a(e, d).wait_recv()
            q = d // 2 * QTR
            pbf[4 * d + e, q : q + QTR] = (part[4 * d + e, q : q + QTR] + rqa[d // 2, e].astype(F32)).astype(BF16)
            near_a(e, d).start()
            far_b(e, d).wait_recv()
            q = HALF + d // 2 * QTR
            pbf[4 * e + d, q : q + QTR] = (part[4 * e + d, q : q + QTR] + rqb[d // 2, e].astype(F32)).astype(BF16)
            near_b(e, d).start()

    for e in (2, 1, 3, 0):
        near_sends(e)

    def sib(buf, rec, base, d):
        return rc(buf.at[d], rec.at[d], x_s.at[base + d], x_r.at[base + d], dev(dc=1))

    def xfar(buf, rec, base, d):
        h = pl.ds(d // 2 * HALF, HALF)
        return rc(buf.at[2, h], rec.at[0, h], x_s.at[base + d], x_r.at[base + d], dev(dx=d))

    def xnear(buf, rec, base, d):
        return rc(buf.at[d], rec.at[d], x_s.at[base + 3 + d], x_r.at[base + 3 + d], dev(dx=d))

    for d in (2, 1, 3, 0):
        tsib[d] = tgrad[pl.ds((2 * d + 1) * ROWS, ROWS)].astype(BF16)
        sib(tsib, trec, 0, d).start()

    def owner_grad(b):
        spots = column(b)
        both = jnp.concatenate([spots, spots], axis=0)
        return mm(both, sgr[b].reshape(2 * ROWS, D), TN)

    for d in (2, 1, 3):
        sib(tsib, trec, 0, d).wait_recv()
        share = tgrad[pl.ds(2 * d * ROWS, ROWS)] + trec[d].astype(F32)
        if d == 2:
            tsx[2] = share.astype(BF16)
            for e in (1, 3):
                xfar(tsx, trx, 8, e).start()
        else:
            tgrad[pl.ds(2 * d * ROWS, ROWS)] = share
    for d in (2, 1, 3, 0):
        csib[d] = owner_grad(2 * d + 1).astype(BF16)
        sib(csib, crec, 4, d).start()
    own_c = {}
    for d in (2, 1, 3):
        own_c[d] = owner_grad(2 * d)
        sib(csib, crec, 4, d).wait_recv()
        own_c[d] = own_c[d] + crec[d].astype(F32)
        if d == 2:
            csx[2] = own_c[2].astype(BF16)
            for e in (1, 3):
                xfar(csx, crx, 16, e).start()
    for d in (1, 3):
        xfar(tsx, trx, 8, d).wait_recv()
        h = d // 2 * HALF
        tsx[d] = tgrad[pl.ds(2 * d * ROWS, ROWS)].astype(BF16)
        tsx[d, h : h + HALF] = (tgrad[pl.ds(2 * d * ROWS + h, HALF)] + trx[0, h : h + HALF].astype(F32)).astype(BF16)
        xnear(tsx, trx, 8, d).start()
    for d in (1, 3):
        xfar(csx, crx, 16, d).wait_recv()
        h = d // 2 * HALF
        csx[d] = own_c[d].astype(BF16)
        csx[d, h : h + HALF] = (own_c[d][h : h + HALF] + crx[0, h : h + HALF].astype(F32)).astype(BF16)
        xnear(csx, crx, 16, d).start()

    def line(w, d):
        return dev(0, d) if w == 0 else dev(d)

    def ufar(w, d):
        q = pl.ds(d // 2 * QTR, QTR)
        return rc(usend.at[w, 2, q], uq.at[w, q], u_s.at[w, d], u_r.at[w, d], line(w, d))

    def unear(w, d):
        return rc(usend.at[w, d], uh.at[w, d], u_s.at[w, 4 + d], u_r.at[w, 4 + d], line(w, d))

    for e in (2, 1, 3, 0):
        for w in (0, 1):
            at, top = (e, 0) if w == 0 else (4 * e, HALF)
            near, rec = (near_a, rha) if w == 0 else (near_b, rhb)
            for d in (1, 3):
                near(e, d).wait_recv()
            total = part[at, top : top + HALF] + rec[0, e].astype(F32) + rec[1, e].astype(F32)
            if e == 2:
                usend[w, 2] = total.astype(BF16)
                for d in (1, 3):
                    ufar(w, d).start()
            elif e:
                ufar(w, e).wait_recv()
                usend[w, e] = total.astype(BF16)
                q = e // 2 * QTR
                usend[w, e, q : q + QTR] = (total[q : q + QTR] + uq[w, q : q + QTR].astype(F32)).astype(BF16)
                unear(w, e).start()
            else:
                part[0, top : top + HALF] = total

    sib(tsib, trec, 0, 0).wait_recv()
    for d in (1, 3):
        xnear(tsx, trx, 8, d).wait_recv()
    tg_out[...] = tgrad[0:ROWS] + trec[0].astype(F32) + trx[1].astype(F32) + trx[3].astype(F32)
    own = owner_grad(0)
    sib(csib, crec, 4, 0).wait_recv()
    for d in (1, 3):
        xnear(csx, crx, 16, d).wait_recv()
    cg_out[...] = own + crec[0].astype(F32) + crx[1].astype(F32) + crx[3].astype(F32)
    for w in (0, 1):
        for d in (1, 3):
            unear(w, d).wait_recv()
        top = w * HALF
        ig_out[top : top + HALF] = part[0, top : top + HALF] + uh[w, 1].astype(F32) + uh[w, 3].astype(F32)

    for d in (1, 3):
        a_y(d).wait_send()
        b_z(d).wait_send()
        aq_y(d).wait_send()
        bq_z(d).wait_send()
        for e in range(4):
            a_z(e, d).wait_send()
            b_y(e, d).wait_send()
            aq_z(e, d).wait_send()
            bq_y(e, d).wait_send()
            far_a(e, d).wait_send()
            far_b(e, d).wait_send()
            near_a(e, d).wait_send()
            near_b(e, d).wait_send()
        for ref, ss, sr in ((txt, t_s, t_r), (cac, c_s, c_r)):
            along_x(ref, ss, sr, d).wait_send()
            half_x(ref, ss, sr, d).wait_send()
        tbl_y(d).wait_send()
        tbl_z(d).wait_send()
        for buf, rec, base in ((tsx, trx, 8), (csx, crx, 16)):
            xfar(buf, rec, base, d).wait_send()
            xnear(buf, rec, base, d).wait_send()
        for w in (0, 1):
            ufar(w, d).wait_send()
            unear(w, d).wait_send()
    tbl_y2().wait_send()
    tbl_z2().wait_send()
    for d in range(4):
        to_sib(txt, t_s, t_r, d).wait_send()
        to_sib(cac, c_s, c_r, d).wait_send()
        sib(tsib, trec, 0, d).wait_send()
        sib(csib, crec, 4, d).wait_send()


def place_out(a, b, c, a_out, b_out, c_out, held, sems):
    ways = tuple(enumerate(((a, a_out), (b, b_out), (c, c_out))))
    into = [pltpu.make_async_copy(s, held.at[n], sems.at[n]) for n, (s, _) in ways]
    out = [pltpu.make_async_copy(held.at[n], t, sems.at[3 + n]) for n, (_, t) in ways]
    for copy in into:
        copy.start()
    for first, then in zip(into, out):
        first.wait()
        then.start()
    for copy in out:
        copy.wait()


def shards(images, texts, cache, mate_owner, mate_row, mate_count, log_scale, bias):
    vm = pl.BlockSpec(memory_space=pltpu.VMEM)
    dma = pltpu.SemaphoreType.DMA
    out = jax.ShapeDtypeStruct((ROWS, D), F32)
    four = lambda rows: pltpu.VMEM((4, rows, D), BF16)
    grads = (
        pl.pallas_call(
            kernel,
            out_shape=(out, out, out),
            in_specs=[vm] * 8,
            out_specs=(vm, vm, vm),
            scratch_shapes=[
                pltpu.VMEM((16, ROWS, D), BF16),
                pltpu.VMEM((8 * ROWS, D), BF16),
                pltpu.VMEM((8 * ROWS, D), BF16),
                pltpu.VMEM((8, ROWS, D), BF16),
                pltpu.VMEM((4, 4, 16, ROWS), I32),
                pltpu.VMEM((2 * ROWS, 8 * ROWS), BF16),
                pltpu.VMEM((8 * ROWS, D), F32),
                pltpu.VMEM((16, ROWS, D), F32),
                pltpu.VMEM((16, ROWS, D), BF16),
                pltpu.VMEM((8, 2, ROWS, D), BF16),
                pltpu.VMEM((2, 4, QTR, D), BF16),
                pltpu.VMEM((2, 4, QTR, D), BF16),
                pltpu.VMEM((2, 4, HALF, D), BF16),
                pltpu.VMEM((2, 4, HALF, D), BF16),
                pltpu.VMEM((2, 4, HALF, D), BF16),
                pltpu.VMEM((2, HALF, D), BF16),
                pltpu.VMEM((2, 4, HALF, D), BF16),
                four(ROWS), four(ROWS), four(ROWS), four(ROWS),
                four(ROWS), four(ROWS), four(ROWS), four(ROWS),
                dma((4, 4)), dma((4, 4)), dma((4, 4)), dma((4, 4)),
                dma((2, 5)), dma((2, 5)), dma((2, 5)), dma((2, 5)),
                dma((12,)), dma((12,)), dma((12,)), dma((12,)),
                dma((8,)), dma((8,)),
                dma((2, 4)), dma((2, 4)), dma((2, 4)), dma((2, 4)),
                dma((2, 4)), dma((2, 4)), dma((2, 4)), dma((2, 4)),
                dma((2, 8)), dma((2, 8)), dma((24,)), dma((24,)),
            ],
            compiler_params=pltpu.CompilerParams(
                collective_id=0, has_side_effects=True, vmem_limit_bytes=62 << 20
            ),
            cost_estimate=pl.CostEstimate(flops=17_000_000_000, bytes_accessed=4_000_000, transcendentals=2_000_000),
        )(
            log_scale.reshape(1, 1), bias.reshape(1, 1), images, texts, cache,
            mate_owner.T, mate_row.T, mate_count.reshape(1, ROWS),
        )
    )
    anywhere = pl.BlockSpec(memory_space=pl.ANY)
    return tuple(
        pl.pallas_call(
            place_out,
            out_shape=(out, out, out),
            in_specs=[anywhere] * 3,
            out_specs=(anywhere,) * 3,
            scratch_shapes=[pltpu.VMEM((3, ROWS, D), F32), dma((6,))],
        )(*grads)
    )


def solution(mesh):
    rows = P(("blk", "img"), None)
    return jax.shard_map(
        shards,
        mesh=mesh,
        in_specs=(rows, rows, rows, rows, rows, P(("blk", "img")), P(), P()),
        out_specs=(rows, rows, rows),
        check_vma=False,
    )
```

time: 117 us -> 106 us (0.906)
  local copies, waits for them, and re-layouts: 6.23 us -> 0 us
  Pallas kernels: 108 us -> 104 us
    pallas_call x1, Pallas kernels: 108 us -> 101 us  [shards(): pl.pallas_call(kernel, out_shape=(out, out, out), in_specs=[vm] * 8, out_...]
    unnamed x13 -> x0, local copies, waits for them, and re-layouts: 6.23 us -> none
    pallas_call x0 -> x1, Pallas kernels: none -> 2.32 us  [shards(): pl.pallas_call(place_out, out_shape=(out, out, out), in_specs=[anywhere]...]
where the time goes in v2:
time: 106 us
  Pallas kernels  104 us (98%)
  between operations  1.93 us (2%)
    pallas_call x1, Pallas kernels, shards(): pl.pallas_call(kernel, out_shape=(out, out, out), in_specs=[vm] * 8, out_...  101 us
    pallas_call x1, Pallas kernels, shards(): pl.pallas_call(place_out, out_shape=(out, out, out), in_specs=[anywhere]...  2.32 us

profile of v2, /device:TPU:1, one launch (start us, length us, event | category | flops | bytes accessed | tf_op | source)
XLA Modules:
  0.0 105.5 jit_solution(5184403867512500803)
XLA Ops:
  1.9 101.3 %shard_map.103 = (f32[128,1152]{1,0:T(8,128)}, f32[128,1152]{1,0:T(8,128)}, f32[128,1152]{1,0:T(8,128)}) custom-call(f32[1,1]{1,0:T(1,128)} %bitcast.5.ls_ref, f32[1,1]{1,0:T(1,128)} %bitcast.6.bias_ref, bf16[128,1152]{1,0:T(8,128)(2,1)} %images.1, bf16[128,1152]{1,0:T(8,128)(2,1)} %texts.1, bf16[128,1152]{1,0:T(8,128)(2,1)} %cache.1, s32[4,128]{1,0:T(4,128)} %bitcast.7, ...), custom_call_target="tpu_custom_call" | custom-call | flops 16999999488 | bytes 4000000 | tf_op jit(solution)/shard_map/pallas_call | solution.py:534
  103.2 2.3 %shard_map.104 = (f32[128,1152]{1,0:T(8,128)}, f32[128,1152]{1,0:T(8,128)}, f32[128,1152]{1,0:T(8,128)}) custom-call(f32[128,1152]{1,0:T(8,128)} %get-tuple-element.6.a, f32[128,1152]{1,0:T(8,128)} %get-tuple-element.7.b, f32[128,1152]{1,0:T(8,128)} %get-tuple-element.8.c), custom_call_target="tpu_custom_call" | custom-call | tf_op jit(solution)/shard_map/pallas_call | solution.py:578

commit v3 on v1

v3 whole, which is shorter than its diff:
```python
import jax
import jax.numpy as jnp
from jax import lax
from jax.experimental import pallas as pl
from jax.experimental.pallas import tpu as pltpu
from jax.sharding import PartitionSpec as P

MESH = pl.DeviceIdType.MESH
F32, BF16, I32 = jnp.float32, jnp.bfloat16, jnp.int32
NT = (((1,), (1,)), ((), ()))
NN = (((1,), (0,)), ((), ()))
TN = (((0,), (0,)), ((), ()))
ROWS, D, HALF, QTR = 128, 1152, 64, 32
ORDER = ((1, 0), (1, 1), (0, 2), (1, 2), (0, 1), (1, 3), (0, 3), (0, 0))
SLAB = {key: n for n, key in enumerate(ORDER)}


def mm(a, b, dims):
    return lax.dot_general(a, b, dims, preferred_element_type=F32)


def kernel(
    ls_ref, bias_ref, images, texts, cache, owner, row, count,
    ig_out, tg_out, cg_out,
    img, txt, cac, gat, tbl, coeff, tgrad, part, pbf, sgr,
    rq, rh, usend, uq, uh, tsib, trec, csib, crec, tsx, trx, csx, crx, cgrad,
    h_s, h_r, q_s, q_r, t_s, t_r, c_s, c_r, k_s, k_r,
    rq_s, rq_r, rh_s, rh_r, u_s, u_r, x_s, x_r,
):
    blk, im = lax.axis_index("blk"), lax.axis_index("img")
    z, y, x, c = blk // 8, (blk // 2) % 4, (blk % 2) * 2 + im // 2, im % 2

    def dev(dz=0, dy=0, dx=0, dc=0):
        zz, yy, xx = (z + dz + 4) % 4, (y + dy + 4) % 4, (x + dx + 4) % 4
        return ((zz * 4 + yy) * 2 + xx // 2, (xx % 2) * 2 + (c + dc) % 2)

    def rc(src, dst, ss, rs, to):
        return pltpu.make_async_remote_copy(
            src_ref=src, dst_ref=dst, send_sem=ss, recv_sem=rs, device_id=to, device_id_type=MESH
        )

    def outer_dev(h, d):
        return dev(d) if h else dev(0, d)

    def inner_dev(h, d):
        return dev(0, d) if h else dev(d)

    def quarter(d):
        return pl.ds(d // 2 * QTR, QTR)

    def go_out(h, d):
        return rc(img.at[SLAB[h, 0], 0], img.at[SLAB[h, d], 0], h_s.at[h, d, 0], h_r.at[h, d, 0], outer_dev(h, -d))

    def go_out_q(h, d):
        q = quarter(d)
        return rc(img.at[SLAB[h, d], 0, q], img.at[SLAB[h, 2], 0, q],
                  q_s.at[h, d // 2, 4], q_r.at[h, d // 2, 4], outer_dev(h, -d))

    def go_in(h, o, d):
        return rc(img.at[SLAB[h, o], 0], img.at[SLAB[h, o], d], h_s.at[h, o, d], h_r.at[h, o, d], inner_dev(h, -d))

    def go_in_q(h, o, d):
        q = quarter(d)
        return rc(img.at[SLAB[h, o], d, q], img.at[SLAB[h, o], 2, q],
                  q_s.at[h, d // 2, o], q_r.at[h, d // 2, o], inner_dev(h, -d))

    def rows_of(ref, n):
        return ref.at[pl.ds(n * ROWS, ROWS)]

    def along_x(ref, sems, semr, d):
        return rc(rows_of(ref, 0), rows_of(ref, 2 * d), sems.at[2 * d], semr.at[2 * d], dev(dx=-d))

    def half_x(ref, sems, semr, d):
        h = d // 2 * HALF
        return rc(ref.at[pl.ds(2 * d * ROWS + h, HALF)], ref.at[pl.ds(4 * ROWS + h, HALF)],
                  sems.at[8 + d], semr.at[8 + d], dev(dx=-d))

    def to_sib(ref, sems, semr, d):
        return rc(rows_of(ref, 2 * d), rows_of(ref, 2 * d + 1), sems.at[2 * d + 1], semr.at[2 * d + 1], dev(dc=1))

    def tbl_to(dz, dy):
        return rc(tbl.at[0, 0], tbl.at[dz, dy], k_s.at[dz, dy], k_r.at[dz, dy], dev(-dz, -dy))

    plane = [(dz, dy) for dz in range(4) for dy in range(4) if dz or dy]
    peers = [dev(dz, dy) for dz, dy in plane] + [dev(dx=1), dev(dx=3), dev(dc=1)]
    barrier = pltpu.get_barrier_semaphore()
    for to in peers:
        pl.semaphore_signal(barrier, inc=1, device_id=to, device_id_type=MESH)
    for h in (0, 1):
        img[SLAB[h, 0], 0] = images[h * HALF : h * HALF + HALF]
    txt[0:ROWS] = texts[...]
    cac[0:ROWS] = cache[...]
    lane = lax.broadcasted_iota(I32, (ROWS, ROWS), 1)
    sub = lax.broadcasted_iota(I32, (ROWS, ROWS), 0)
    below = (sub > lane).astype(BF16)

    def down(line):
        return jnp.transpose(jnp.broadcast_to(line.astype(F32), (ROWS, ROWS)))

    live = down(count[...])
    carry = jnp.zeros((1, ROWS), F32)
    picked_r = [jnp.zeros((1, ROWS), F32) for _ in range(8)]
    picked_c = [jnp.zeros((1, ROWS), F32) for _ in range(8)]
    row1 = (sub + 1).astype(F32)
    for k in range(4):
        hits = ((down(owner[k : k + 1, :]) == lane.astype(F32)) & (live > k)).astype(F32)
        rank = mm(below, hits.astype(BF16), NN) + carry
        carry = carry + jnp.sum(hits, axis=0, keepdims=True)
        cols = down(row[k : k + 1, :])
        for s in range(8):
            sel = jnp.where(rank == s, hits, 0.0)
            picked_r[s] = picked_r[s] + jnp.sum(sel * row1, axis=0, keepdims=True)
            picked_c[s] = picked_c[s] + jnp.sum(sel * cols, axis=0, keepdims=True)
    for s in range(8):
        tbl[0, 0, s : s + 1, :] = picked_r[s].astype(I32)
        tbl[0, 0, 8 + s : 9 + s, :] = picked_c[s].astype(I32)
    pl.semaphore_wait(barrier, len(peers))
    for dz, dy in plane:
        tbl_to(dz, dy).start()

    for d in (1, 3):
        for h in (0, 1):
            go_out(h, d).start()
        along_x(cac, c_s, c_r, d).start()
    to_sib(cac, c_s, c_r, 0).start()
    for d in (1, 3):
        for h in (0, 1):
            go_in(h, 0, d).start()

    for d in (1, 3):
        for h in (0, 1):
            go_out(h, d).wait_recv()
            go_out_q(h, d).start()
            for e in (1, 3):
                go_in(h, d, e).start()
    for d in (1, 3):
        along_x(cac, c_s, c_r, d).wait_recv()
        half_x(cac, c_s, c_r, d).start()
        to_sib(cac, c_s, c_r, d).start()
    for d in (1, 3):
        along_x(txt, t_s, t_r, d).start()
    to_sib(txt, t_s, t_r, 0).start()
    for d in (1, 3):
        for h in (0, 1):
            go_in(h, 0, d).wait_recv()
            go_in_q(h, 0, d).start()
    tgrad[...] = jnp.zeros_like(tgrad)
    for h in (0, 1):
        for d in (1, 3):
            go_out_q(h, d).wait_recv()
        for d in (1, 3):
            go_in(h, 2, d).start()
    for d in (1, 3):
        half_x(cac, c_s, c_r, d).wait_recv()
    to_sib(cac, c_s, c_r, 2).start()
    for dz, dy in plane:
        tbl_to(dz, dy).wait_recv()

    scale = jnp.exp(ls_ref[...])
    half = 0.5 * scale
    shift = 0.5 * bias_ref[...]

    def text_step(t):
        mine = img[t].reshape(2 * ROWS, D)
        logit = mm(mine, txt[...], NT)
        coeff[...] = (half + half * jnp.tanh(half * logit + shift)).astype(BF16)

        for h in (0, 1):
            @pl.when(t == SLAB[h, 0])
            def _():
                own = mm(img[SLAB[h, 0], 0], txt[0:ROWS], NT)
                prob = half + half * jnp.tanh(half * own + shift)
                same = sub[0:HALF] + h * HALF == lane[0:HALF]
                coeff[0:HALF, 0:ROWS] = (prob - jnp.where(same, scale, 0.0)).astype(BF16)

        co = coeff[...]
        total = part[t] + mm(co, txt[...], NN).reshape(4, HALF, D)
        part[t] = total
        pbf[t] = total.astype(BF16)
        tgrad[...] += mm(co, mine, TN)

    def spread_lanes(table, first):
        want = lax.broadcasted_iota(I32, (ROWS, ROWS), 0)
        b = lax.broadcasted_iota(I32, (ROWS, ROWS), 1) // 16
        of = first + ((x + b // 2) % 4) * 2 + (c + b) % 2
        return mm(table, (want == of).astype(BF16), NN)

    first = (z * 4 + y) * 8
    tab = tbl[...].reshape(16, 2, 8, ROWS)
    tab_r = tab[:, 0].reshape(ROWS, ROWS).astype(F32).astype(BF16)
    tab_c = tab[:, 1].reshape(ROWS, ROWS).astype(F32).astype(BF16)

    def column(b):
        of = first + ((x + b // 2) % 4) * 2 + (c + b) % 2
        want = lax.broadcasted_iota(I32, (ROWS, ROWS), 0)
        return (mm(tab_c, (want == of).astype(BF16), NN) == lane.astype(F32)).astype(BF16)

    lanes_r = spread_lanes(tab_r, first)

    def gather_rows():
        for d in range(4):
            to_sib(cac, c_s, c_r, d).wait_recv()
        for b in range(8):
            gat[b] = mm(column(b), cac[pl.ds(b * ROWS, ROWS)], NN).astype(BF16)

    def far(h, o, d):
        return rc(pbf.at[SLAB[h, o], 2, quarter(d)], rq.at[h, d // 2, o],
                  rq_s.at[h, d // 2, o], rq_r.at[h, d // 2, o], inner_dev(h, d))

    def near(h, o, d):
        return rc(pbf.at[SLAB[h, o], d], rh.at[h, d // 2, o],
                  rh_s.at[h, d // 2, o], rh_r.at[h, d // 2, o], inner_dev(h, d))

    def ufar(h, d):
        return rc(usend.at[h, 2, quarter(d)], uq.at[h, quarter(d)], u_s.at[h, d], u_r.at[h, d], outer_dev(h, d))

    def unear(h, d):
        return rc(usend.at[h, d], uh.at[h, d], u_s.at[h, 4 + d], u_r.at[h, 4 + d], outer_dev(h, d))

    def far_sends(h, o):
        for d in (1, 3):
            far(h, o, d).start()

    def near_sends(h, o):
        n = SLAB[h, o]
        for d in (1, 3):
            far(h, o, d).wait_recv()
            q = d // 2 * QTR
            pbf[n, d, q : q + QTR] = (part[n, d, q : q + QTR] + rq[h, d // 2, o].astype(F32)).astype(BF16)
            near(h, o, d).start()

    def inner_sum(h, o):
        n = SLAB[h, o]
        for d in (1, 3):
            near(h, o, d).wait_recv()
        total = part[n, 0] + rh[h, 0, o].astype(F32) + rh[h, 1, o].astype(F32)
        if o == 2:
            usend[h, 2] = total.astype(BF16)
            for d in (1, 3):
                ufar(h, d).start()
        else:
            part[n, 0] = total

    def outer_send(h, o):
        n, q = SLAB[h, o], o // 2 * QTR
        ufar(h, o).wait_recv()
        usend[h, o] = part[n, 0].astype(BF16)
        usend[h, o, q : q + QTR] = (part[n, 0, q : q + QTR] + uq[h, q : q + QTR].astype(F32)).astype(BF16)
        unear(h, o).start()

    def mate_step(dz, p):
        pair = dz * 2 + p
        mine = jnp.concatenate(
            [img[SLAB[0, 2 * p], dz], img[SLAB[0, 2 * p + 1], dz], img[SLAB[1, dz], 2 * p], img[SLAB[1, dz], 2 * p + 1]],
            axis=0,
        )
        emb = gat[:, pair * 16 : pair * 16 + 16, :].reshape(ROWS, D)
        keep = jnp.where(sub == pair * 16 + lane % 16, lanes_r, 0.0)
        at_row = jnp.sum(keep, axis=0, keepdims=True)
        big_sub = lax.broadcasted_iota(I32, (2 * ROWS, ROWS), 0)
        second = lax.broadcasted_iota(I32, (1, ROWS), 1) % 16 // 8
        moved = jnp.where(at_row > HALF + 0.5, 64.0, 0.0) + second.astype(F32) * HALF
        target = jnp.where(at_row > 0.5, at_row - 1.0 + moved, -1.0)
        named = big_sub.astype(F32) == target
        logit = mm(mine, emb, NT)
        wt = jnp.where(named, half * jnp.tanh(half * logit + shift) - half, 0.0).astype(BF16)
        grad = mm(wt, emb, NN)
        part[SLAB[0, 2 * p], dz] = grad[0:HALF]
        part[SLAB[0, 2 * p + 1], dz] = grad[HALF:ROWS]
        part[SLAB[1, dz], 2 * p] = grad[ROWS : ROWS + HALF]
        part[SLAB[1, dz], 2 * p + 1] = grad[ROWS + HALF :]
        slots = mm(wt, mine, TN)
        top = slots.astype(BF16)
        sgr[:, 0, pair * 16 : pair * 16 + 16, :] = top.reshape(8, 16, D)
        sgr[:, 1, pair * 16 : pair * 16 + 16, :] = (slots - top.astype(F32)).astype(BF16).reshape(8, 16, D)
    def in_quarters(h, o):
        for d in (1, 3):
            go_in_q(h, o, d).wait_recv()

    gather_rows()
    mate_step(0, 0)
    for o in (1, 3):
        for h in (0, 1):
            for d in (1, 3):
                go_in(h, o, d).wait_recv()
                go_in_q(h, o, d).start()
    mate_step(1, 0)
    mate_step(3, 0)
    in_quarters(1, 0)
    mate_step(0, 1)
    for d in (1, 3):
        along_x(txt, t_s, t_r, d).wait_recv()
        half_x(txt, t_s, t_r, d).start()
        to_sib(txt, t_s, t_r, d).start()
    for h in (0, 1):
        for d in (1, 3):
            go_in(h, 2, d).wait_recv()
            go_in_q(h, 2, d).start()
    in_quarters(1, 1)
    mate_step(1, 1)
    in_quarters(1, 3)
    mate_step(3, 1)
    for d in (1, 3):
        half_x(txt, t_s, t_r, d).wait_recv()
    to_sib(txt, t_s, t_r, 2).start()
    for d in range(4):
        to_sib(txt, t_s, t_r, d).wait_recv()

    def sib(buf, rec, base, d):
        return rc(buf.at[d], rec.at[d], x_s.at[base + d], x_r.at[base + d], dev(dc=1))

    def xfar(buf, rec, base, d):
        h = pl.ds(d // 2 * HALF, HALF)
        return rc(buf.at[2, h], rec.at[0, h], x_s.at[base + d], x_r.at[base + d], dev(dx=d))

    def xnear(buf, rec, base, d):
        return rc(buf.at[d], rec.at[d], x_s.at[base + 3 + d], x_r.at[base + 3 + d], dev(dx=d))

    def owner_grad(b):
        spots = column(b)
        both = jnp.concatenate([spots, spots], axis=0)
        return mm(both, sgr[b].reshape(2 * ROWS, D), TN)

    def cache_to_sibling():
        for d in (2, 1, 3, 0):
            csib[d] = owner_grad(2 * d + 1).astype(BF16)
            sib(csib, crec, 4, d).start()

    def cache_far_sends():
        for d in (2, 1, 3, 0):
            cgrad[d] = owner_grad(2 * d)
            sib(csib, crec, 4, d).wait_recv()
            cgrad[d] += crec[d].astype(F32)
            if d == 2:
                csx[2] = cgrad[2].astype(BF16)
                for e in (1, 3):
                    xfar(csx, crx, 16, e).start()

    def cache_near_sends():
        for d in (1, 3):
            xfar(csx, crx, 16, d).wait_recv()
            h = d // 2 * HALF
            csx[d] = cgrad[d].astype(BF16)
            csx[d, h : h + HALF] = (cgrad[d, h : h + HALF] + crx[0, h : h + HALF].astype(F32)).astype(BF16)
            xnear(csx, crx, 16, d).start()

    def cache_result():
        for d in (1, 3):
            xnear(csx, crx, 16, d).wait_recv()
        cg_out[...] = cgrad[0] + crx[1].astype(F32) + crx[3].astype(F32)

    def step(t, carried):
        @pl.when(t == 2)
        def _():
            in_quarters(0, 0)
            in_quarters(0, 1)
            mate_step(2, 0)
            in_quarters(0, 2)
            in_quarters(0, 3)
            in_quarters(1, 2)
            mate_step(2, 1)
            cache_to_sibling()

        text_step(t)
        for n in range(8):
            @pl.when(t == n)
            def _():
                far_sends(*ORDER[n])
                if n >= 2:
                    near_sends(*ORDER[n - 2])
                if n == 2:
                    cache_far_sends()
                if n >= 4:
                    inner_sum(*ORDER[n - 4])
                if n == 4:
                    cache_near_sends()

        return carried

    lax.fori_loop(0, 8, step, 0)

    for d in (2, 1, 3, 0):
        tsib[d] = tgrad[(2 * d + 1) * ROWS : (2 * d + 2) * ROWS].astype(BF16)
        sib(tsib, trec, 0, d).start()
    near_sends(*ORDER[6])
    inner_sum(*ORDER[4])
    outer_send(0, 1)
    sib(tsib, trec, 0, 2).wait_recv()
    tsx[2] = (tgrad[4 * ROWS : 5 * ROWS] + trec[2].astype(F32)).astype(BF16)
    for e in (1, 3):
        xfar(tsx, trx, 8, e).start()
    outer_send(1, 1)
    inner_sum(*ORDER[5])
    outer_send(1, 3)
    near_sends(*ORDER[7])
    for d in (1, 3):
        h = d // 2 * HALF
        sib(tsib, trec, 0, d).wait_recv()
        share = tgrad[2 * d * ROWS : (2 * d + 1) * ROWS] + trec[d].astype(F32)
        tgrad[2 * d * ROWS : (2 * d + 1) * ROWS] = share
        tsx[d] = share.astype(BF16)
        xfar(tsx, trx, 8, d).wait_recv()
        tsx[d, h : h + HALF] = (
            tgrad[2 * d * ROWS + h : 2 * d * ROWS + h + HALF] + trx[0, h : h + HALF].astype(F32)
        ).astype(BF16)
        xnear(tsx, trx, 8, d).start()
    inner_sum(*ORDER[6])
    outer_send(0, 3)
    cache_result()
    inner_sum(*ORDER[7])
    for h in (1, 0):
        for d in (1, 3):
            unear(h, d).wait_recv()
        ig_out[h * HALF : h * HALF + HALF] = part[SLAB[h, 0], 0] + uh[h, 1].astype(F32) + uh[h, 3].astype(F32)
    sib(tsib, trec, 0, 0).wait_recv()
    for d in (1, 3):
        xnear(tsx, trx, 8, d).wait_recv()
    tg_out[...] = tgrad[0:ROWS] + trec[0].astype(F32) + trx[1].astype(F32) + trx[3].astype(F32)

    for d in (1, 3):
        for h in (0, 1):
            go_out(h, d).wait_send()
            go_out_q(h, d).wait_send()
            for o in range(4):
                go_in(h, o, d).wait_send()
                go_in_q(h, o, d).wait_send()
                far(h, o, d).wait_send()
                near(h, o, d).wait_send()
            ufar(h, d).wait_send()
            unear(h, d).wait_send()
        for ref, ss, sr in ((txt, t_s, t_r), (cac, c_s, c_r)):
            along_x(ref, ss, sr, d).wait_send()
            half_x(ref, ss, sr, d).wait_send()
        for buf, rec, base in ((tsx, trx, 8), (csx, crx, 16)):
            xfar(buf, rec, base, d).wait_send()
            xnear(buf, rec, base, d).wait_send()
    for dz, dy in plane:
        tbl_to(dz, dy).wait_send()
    for d in range(4):
        to_sib(txt, t_s, t_r, d).wait_send()
        to_sib(cac, c_s, c_r, d).wait_send()
        sib(tsib, trec, 0, d).wait_send()
        sib(csib, crec, 4, d).wait_send()


def place_out(a, b, c, a_out, b_out, c_out, held, sems):
    ways = tuple(enumerate(((a, a_out), (b, b_out), (c, c_out))))
    into = [pltpu.make_async_copy(s, held.at[n], sems.at[n]) for n, (s, _) in ways]
    out = [pltpu.make_async_copy(held.at[n], t, sems.at[3 + n]) for n, (_, t) in ways]
    for copy in into:
        copy.start()
    for first, then in zip(into, out):
        first.wait()
        then.start()
    for copy in out:
        copy.wait()


def shards(images, texts, cache, mate_owner, mate_row, mate_count, log_scale, bias):
    vm = pl.BlockSpec(memory_space=pltpu.VMEM)
    dma = pltpu.SemaphoreType.DMA
    out = jax.ShapeDtypeStruct((ROWS, D), F32)
    four = lambda rows: pltpu.VMEM((4, rows, D), BF16)
    grads = (
        pl.pallas_call(
            kernel,
            out_shape=(out, out, out),
            in_specs=[vm] * 8,
            out_specs=(vm, vm, vm),
            scratch_shapes=[
                pltpu.VMEM((8, 4, HALF, D), BF16),
                pltpu.VMEM((8 * ROWS, D), BF16),
                pltpu.VMEM((8 * ROWS, D), BF16),
                pltpu.VMEM((8, ROWS, D), BF16),
                pltpu.VMEM((4, 4, 16, ROWS), I32),
                pltpu.VMEM((2 * ROWS, 8 * ROWS), BF16),
                pltpu.VMEM((8 * ROWS, D), F32),
                pltpu.VMEM((8, 4, HALF, D), F32),
                pltpu.VMEM((8, 4, HALF, D), BF16),
                pltpu.VMEM((8, 2, ROWS, D), BF16),
                pltpu.VMEM((2, 2, 4, QTR, D), BF16),
                pltpu.VMEM((2, 2, 4, HALF, D), BF16),
                pltpu.VMEM((2, 4, HALF, D), BF16),
                pltpu.VMEM((2, HALF, D), BF16),
                pltpu.VMEM((2, 4, HALF, D), BF16),
                four(ROWS), four(ROWS), four(ROWS), four(ROWS),
                four(ROWS), four(ROWS), four(ROWS), four(ROWS),
                pltpu.VMEM((4, ROWS, D), F32),
                dma((2, 4, 4)), dma((2, 4, 4)), dma((2, 2, 5)), dma((2, 2, 5)),
                dma((12,)), dma((12,)), dma((12,)), dma((12,)),
                dma((4, 4)), dma((4, 4)),
                dma((2, 2, 4)), dma((2, 2, 4)), dma((2, 2, 4)), dma((2, 2, 4)),
                dma((2, 8)), dma((2, 8)), dma((24,)), dma((24,)),
            ],
            compiler_params=pltpu.CompilerParams(
                collective_id=0, has_side_effects=True, vmem_limit_bytes=62 << 20
            ),
            cost_estimate=pl.CostEstimate(flops=17_000_000_000, bytes_accessed=4_000_000, transcendentals=2_000_000),
        )(
            log_scale.reshape(1, 1), bias.reshape(1, 1), images, texts, cache,
            mate_owner.T, mate_row.T, mate_count.reshape(1, ROWS),
        )
    )
    anywhere = pl.BlockSpec(memory_space=pl.ANY)
    return tuple(
        pl.pallas_call(
            place_out,
            out_shape=(out, out, out),
            in_specs=[anywhere] * 3,
            out_specs=(anywhere,) * 3,
            scratch_shapes=[pltpu.VMEM((3, ROWS, D), F32), dma((6,))],
        )(*grads)
    )


def solution(mesh):
    rows = P(("blk", "img"), None)
    return jax.shard_map(
        shards,
        mesh=mesh,
        in_specs=(rows, rows, rows, rows, rows, P(("blk", "img")), P(), P()),
        out_specs=(rows, rows, rows),
        check_vma=False,
    )
```

time: 117 us -> 91.3 us (0.78)
  Pallas kernels: 108 us -> 88.8 us
  local copies, waits for them, and re-layouts: 6.23 us -> 0 us
    pallas_call x1, Pallas kernels: 108 us -> 86.5 us  [shards(): pl.pallas_call(kernel, out_shape=(out, out, out), in_specs=[vm] * 8, out_...]
    unnamed x13 -> x0, local copies, waits for them, and re-layouts: 6.23 us -> none
    pallas_call x0 -> x1, Pallas kernels: none -> 2.32 us  [shards(): pl.pallas_call(place_out, out_shape=(out, out, out), in_specs=[anywhere]...]
where the time goes in v3:
time: 91.3 us; the launch traced here: 90.9 us
  Pallas kernels  88.8 us (97%)
  between operations  2.09 us (2%)
    pallas_call x1, Pallas kernels, shards(): pl.pallas_call(kernel, out_shape=(out, out, out), in_specs=[vm] * 8, out_...  86.5 us
    pallas_call x1, Pallas kernels, shards(): pl.pallas_call(place_out, out_shape=(out, out, out), in_specs=[anywhere]...  2.32 us

profile of v3, /device:TPU:1, one launch (start us, length us, event | category | flops | bytes accessed | tf_op | source)
XLA Modules:
  0.0 90.9 jit_solution(2888225070066205477)
XLA Ops:
  1.9 86.5 %shard_map.103 = (f32[128,1152]{1,0:T(8,128)}, f32[128,1152]{1,0:T(8,128)}, f32[128,1152]{1,0:T(8,128)}) custom-call(f32[1,1]{1,0:T(1,128)} %bitcast.5.ls_ref, f32[1,1]{1,0:T(1,128)} %bitcast.6.bias_ref, bf16[128,1152]{1,0:T(8,128)(2,1)} %images.1, bf16[128,1152]{1,0:T(8,128)(2,1)} %texts.1, bf16[128,1152]{1,0:T(8,128)(2,1)} %cache.1, s32[4,128]{1,0:T(4,128)} %bitcast.7, ...), custom_call_target="tpu_custom_call" | custom-call | flops 16999999488 | bytes 4000000 | tf_op jit(solution)/shard_map/pallas_call | solution.py:465
  88.4 2.3 %shard_map.104 = (f32[128,1152]{1,0:T(8,128)}, f32[128,1152]{1,0:T(8,128)}, f32[128,1152]{1,0:T(8,128)}) custom-call(f32[128,1152]{1,0:T(8,128)} %get-tuple-element.6.a, f32[128,1152]{1,0:T(8,128)} %get-tuple-element.7.b, f32[128,1152]{1,0:T(8,128)} %get-tuple-element.8.c), custom_call_target="tpu_custom_call" | custom-call | tf_op jit(solution)/shard_map/pallas_call | solution.py:506

commit v4 on v3

--- a/solution.py
+++ b/solution.py
@@ -11,7 +11,7 @@
 NN = (((1,), (0,)), ((), ()))
 TN = (((0,), (0,)), ((), ()))
 ROWS, D, HALF, QTR = 128, 1152, 64, 32
-ORDER = ((1, 0), (1, 1), (0, 2), (1, 2), (0, 1), (1, 3), (0, 3), (0, 0))
+ORDER = ((1, 0), (1, 1), (0, 1), (1, 3), (0, 2), (1, 2), (0, 3), (0, 0))
 SLAB = {key: n for n, key in enumerate(ORDER)}
 
 
@@ -121,8 +121,8 @@
     for d in (1, 3):
         for h in (0, 1):
             go_out(h, d).start()
-        along_x(cac, c_s, c_r, d).start()
-    to_sib(cac, c_s, c_r, 0).start()
+        along_x(txt, t_s, t_r, d).start()
+    to_sib(txt, t_s, t_r, 0).start()
     for d in (1, 3):
         for h in (0, 1):
             go_in(h, 0, d).start()
@@ -134,27 +134,33 @@
             for e in (1, 3):
                 go_in(h, d, e).start()
     for d in (1, 3):
-        along_x(cac, c_s, c_r, d).wait_recv()
-        half_x(cac, c_s, c_r, d).start()
-        to_sib(cac, c_s, c_r, d).start()
-    for d in (1, 3):
-        along_x(txt, t_s, t_r, d).start()
-    to_sib(txt, t_s, t_r, 0).start()
-    for d in (1, 3):
         for h in (0, 1):
             go_in(h, 0, d).wait_recv()
             go_in_q(h, 0, d).start()
+    for d in (1, 3):
+        along_x(txt, t_s, t_r, d).wait_recv()
+        half_x(txt, t_s, t_r, d).start()
+        to_sib(txt, t_s, t_r, d).start()
+    for d in (1, 3):
+        along_x(cac, c_s, c_r, d).start()
+    to_sib(cac, c_s, c_r, 0).start()
+    for h in (0, 1):
+        for d in (1, 3):
+            go_out_q(h, d).wait_recv()
+        for d in (1, 3):
+            go_in(h, 2, d).start()
     tgrad[...] = jnp.zeros_like(tgrad)
-    for h in (0, 1):
-        for d in (1, 3):
-            go_out_q(h, d).wait_recv()
-        for d in (1, 3):
-            go_in(h, 2, d).start()
-    for d in (1, 3):
-        half_x(cac, c_s, c_r, d).wait_recv()
-    to_sib(cac, c_s, c_r, 2).start()
+    part[...] = jnp.zeros_like(part)
     for dz, dy in plane:
         tbl_to(dz, dy).wait_recv()
+    for o in (1, 3):
+        for h in (0, 1):
+            for d in (1, 3):
+                go_in(h, o, d).wait_recv()
+                go_in_q(h, o, d).start()
+    for d in (1, 3):
+        half_x(txt, t_s, t_r, d).wait_recv()
+    to_sib(txt, t_s, t_r, 2).start()
 
     scale = jnp.exp(ls_ref[...])
     half = 0.5 * scale
@@ -265,10 +271,10 @@
         logit = mm(mine, emb, NT)
         wt = jnp.where(named, half * jnp.tanh(half * logit + shift) - half, 0.0).astype(BF16)
         grad = mm(wt, emb, NN)
-        part[SLAB[0, 2 * p], dz] = grad[0:HALF]
-        part[SLAB[0, 2 * p + 1], dz] = grad[HALF:ROWS]
-        part[SLAB[1, dz], 2 * p] = grad[ROWS : ROWS + HALF]
-        part[SLAB[1, dz], 2 * p + 1] = grad[ROWS + HALF :]
+        part[SLAB[0, 2 * p], dz] += grad[0:HALF]
+        part[SLAB[0, 2 * p + 1], dz] += grad[HALF:ROWS]
+        part[SLAB[1, dz], 2 * p] += grad[ROWS : ROWS + HALF]
+        part[SLAB[1, dz], 2 * p + 1] += grad[ROWS + HALF :]
         slots = mm(wt, mine, TN)
         top = slots.astype(BF16)
         sgr[:, 0, pair * 16 : pair * 16 + 16, :] = top.reshape(8, 16, D)
@@ -277,32 +283,28 @@
         for d in (1, 3):
             go_in_q(h, o, d).wait_recv()
 
-    gather_rows()
-    mate_step(0, 0)
-    for o in (1, 3):
+    def edges():
         for h in (0, 1):
             for d in (1, 3):
-                go_in(h, o, d).wait_recv()
-                go_in_q(h, o, d).start()
-    mate_step(1, 0)
-    mate_step(3, 0)
-    in_quarters(1, 0)
-    mate_step(0, 1)
-    for d in (1, 3):
-        along_x(txt, t_s, t_r, d).wait_recv()
-        half_x(txt, t_s, t_r, d).start()
-        to_sib(txt, t_s, t_r, d).start()
-    for h in (0, 1):
-        for d in (1, 3):
-            go_in(h, 2, d).wait_recv()
-            go_in_q(h, 2, d).start()
-    in_quarters(1, 1)
-    mate_step(1, 1)
-    in_quarters(1, 3)
-    mate_step(3, 1)
-    for d in (1, 3):
-        half_x(txt, t_s, t_r, d).wait_recv()
-    to_sib(txt, t_s, t_r, 2).start()
+                go_in(h, 2, d).wait_recv()
+                go_in_q(h, 2, d).start()
+
+    def cache_near():
+        for d in (1, 3):
+            along_x(cac, c_s, c_r, d).wait_recv()
+            half_x(cac, c_s, c_r, d).start()
+            to_sib(cac, c_s, c_r, d).start()
+
+    def cache_far():
+        for d in (1, 3):
+            half_x(cac, c_s, c_r, d).wait_recv()
+        to_sib(cac, c_s, c_r, 2).start()
+
+    def send_slab(h, o):
+        n = SLAB[h, o]
+        pbf[n] = part[n].astype(BF16)
+        far_sends(h, o)
+
     for d in range(4):
         to_sib(txt, t_s, t_r, d).wait_recv()
 
@@ -350,29 +352,59 @@
         cg_out[...] = cgrad[0] + crx[1].astype(F32) + crx[3].astype(F32)
 
     def step(t, carried):
+        @pl.when(t == 0)
+        def _():
+            in_quarters(1, 0)
+
+        @pl.when(t == 1)
+        def _():
+            edges()
+            cache_near()
+            in_quarters(1, 1)
+
         @pl.when(t == 2)
         def _():
+            in_quarters(0, 1)
+
+        @pl.when(t == 3)
+        def _():
+            cache_far()
+            in_quarters(1, 3)
+
+        @pl.when(t == 4)
+        def _():
+            gather_rows()
+            mate_step(0, 0)
+            mate_step(0, 1)
+            send_slab(1, 0)
+            mate_step(1, 0)
+            mate_step(1, 1)
+            send_slab(1, 1)
+            mate_step(3, 0)
             in_quarters(0, 0)
-            in_quarters(0, 1)
             mate_step(2, 0)
+            send_slab(0, 1)
+            mate_step(3, 1)
+            send_slab(1, 3)
+            near_sends(1, 0)
             in_quarters(0, 2)
             in_quarters(0, 3)
             in_quarters(1, 2)
             mate_step(2, 1)
             cache_to_sibling()
+            near_sends(1, 1)
 
         text_step(t)
-        for n in range(8):
+        after = {4: ((0, 1), (1, 3)), 5: ((0, 2),), 6: ((1, 2),), 7: ((0, 3),)}
+        for n in range(4, 8):
             @pl.when(t == n)
             def _():
                 far_sends(*ORDER[n])
-                if n >= 2:
-                    near_sends(*ORDER[n - 2])
-                if n == 2:
+                for key in after[n]:
+                    near_sends(*key)
+                if n == 4:
                     cache_far_sends()
-                if n >= 4:
-                    inner_sum(*ORDER[n - 4])
-                if n == 4:
+                if n == 5:
                     cache_near_sends()
 
         return carried
@@ -382,32 +414,32 @@
     for d in (2, 1, 3, 0):
         tsib[d] = tgrad[(2 * d + 1) * ROWS : (2 * d + 2) * ROWS].astype(BF16)
         sib(tsib, trec, 0, d).start()
-    near_sends(*ORDER[6])
-    inner_sum(*ORDER[4])
-    outer_send(0, 1)
     sib(tsib, trec, 0, 2).wait_recv()
     tsx[2] = (tgrad[4 * ROWS : 5 * ROWS] + trec[2].astype(F32)).astype(BF16)
     for e in (1, 3):
         xfar(tsx, trx, 8, e).start()
-    outer_send(1, 1)
-    inner_sum(*ORDER[5])
-    outer_send(1, 3)
-    near_sends(*ORDER[7])
+    inner_sum(0, 2)
+    near_sends(0, 0)
+    inner_sum(1, 2)
     for d in (1, 3):
         h = d // 2 * HALF
         sib(tsib, trec, 0, d).wait_recv()
         share = tgrad[2 * d * ROWS : (2 * d + 1) * ROWS] + trec[d].astype(F32)
-        tgrad[2 * d * ROWS : (2 * d + 1) * ROWS] = share
+        xfar(tsx, trx, 8, d).wait_recv()
         tsx[d] = share.astype(BF16)
-        xfar(tsx, trx, 8, d).wait_recv()
-        tsx[d, h : h + HALF] = (
-            tgrad[2 * d * ROWS + h : 2 * d * ROWS + h + HALF] + trx[0, h : h + HALF].astype(F32)
-        ).astype(BF16)
+        tsx[d, h : h + HALF] = (share[h : h + HALF] + trx[0, h : h + HALF].astype(F32)).astype(BF16)
         xnear(tsx, trx, 8, d).start()
-    inner_sum(*ORDER[6])
+    inner_sum(0, 1)
+    outer_send(0, 1)
+    inner_sum(1, 1)
+    outer_send(1, 1)
+    inner_sum(1, 3)
+    outer_send(1, 3)
+    inner_sum(0, 3)
     outer_send(0, 3)
+    inner_sum(1, 0)
     cache_result()
-    inner_sum(*ORDER[7])
+    inner_sum(0, 0)
     for h in (1, 0):
         for d in (1, 3):
             unear(h, d).wait_recv()

time: 91.3 us -> 90.6 us (level)
  no operation moved by 1% of the time
where the time goes in v4:
time: 90.6 us; the launch traced here: 90.4 us
  Pallas kernels  88.3 us (97%)
  between operations  2.09 us (2%)
    pallas_call x1, Pallas kernels, shards(): pl.pallas_call(kernel, out_shape=(out, out, out), in_specs=[vm] * 8, out_...  86 us
    pallas_call x1, Pallas kernels, shards(): pl.pallas_call(place_out, out_shape=(out, out, out), in_specs=[anywhere]...  2.32 us

profile of v4, /device:TPU:1, one launch (start us, length us, event | category | flops | bytes accessed | tf_op | source)
XLA Modules:
  0.0 90.4 jit_solution(33061188338873251)
XLA Ops:
  1.9 86.0 %shard_map.103 = (f32[128,1152]{1,0:T(8,128)}, f32[128,1152]{1,0:T(8,128)}, f32[128,1152]{1,0:T(8,128)}) custom-call(f32[1,1]{1,0:T(1,128)} %bitcast.5.ls_ref, f32[1,1]{1,0:T(1,128)} %bitcast.6.bias_ref, bf16[128,1152]{1,0:T(8,128)(2,1)} %images.1, bf16[128,1152]{1,0:T(8,128)(2,1)} %texts.1, bf16[128,1152]{1,0:T(8,128)(2,1)} %cache.1, s32[4,128]{1,0:T(4,128)} %bitcast.7, ...), custom_call_target="tpu_custom_call" | custom-call | flops 16999999488 | bytes 4000000 | tf_op jit(solution)/shard_map/pallas_call | solution.py:497
  87.9 2.3 %shard_map.104 = (f32[128,1152]{1,0:T(8,128)}, f32[128,1152]{1,0:T(8,128)}, f32[128,1152]{1,0:T(8,128)}) custom-call(f32[128,1152]{1,0:T(8,128)} %get-tuple-element.6.a, f32[128,1152]{1,0:T(8,128)} %get-tuple-element.7.b, f32[128,1152]{1,0:T(8,128)} %get-tuple-element.8.c), custom_call_target="tpu_custom_call" | custom-call | tf_op jit(solution)/shard_map/pallas_call | solution.py:538

commit v5 on v4

--- a/solution.py
+++ b/solution.py
@@ -23,7 +23,7 @@
     ls_ref, bias_ref, images, texts, cache, owner, row, count,
     ig_out, tg_out, cg_out,
     img, txt, cac, gat, tbl, coeff, tgrad, part, pbf, sgr,
-    rq, rh, usend, uq, uh, tsib, trec, csib, crec, tsx, trx, csx, crx, cgrad,
+    rq, rh, usend, uq, uh, tsib, trec, csib, crec, tsx, trx, csx, crx, cgrad, hot,
     h_s, h_r, q_s, q_r, t_s, t_r, c_s, c_r, k_s, k_r,
     rq_s, rq_r, rh_s, rh_r, u_s, u_r, x_s, x_r,
 ):
@@ -207,7 +207,8 @@
         for d in range(4):
             to_sib(cac, c_s, c_r, d).wait_recv()
         for b in range(8):
-            gat[b] = mm(column(b), cac[pl.ds(b * ROWS, ROWS)], NN).astype(BF16)
+            hot[b] = column(b)
+            gat[b] = mm(hot[b], cac[pl.ds(b * ROWS, ROWS)], NN).astype(BF16)
 
     def far(h, o, d):
         return rc(pbf.at[SLAB[h, o], 2, quarter(d)], rq.at[h, d // 2, o],
@@ -319,7 +320,7 @@
         return rc(buf.at[d], rec.at[d], x_s.at[base + 3 + d], x_r.at[base + 3 + d], dev(dx=d))
 
     def owner_grad(b):
-        spots = column(b)
+        spots = hot[b]
         both = jnp.concatenate([spots, spots], axis=0)
         return mm(both, sgr[b].reshape(2 * ROWS, D), TN)
 
@@ -518,6 +519,7 @@
                 four(ROWS), four(ROWS), four(ROWS), four(ROWS),
                 four(ROWS), four(ROWS), four(ROWS), four(ROWS),
                 pltpu.VMEM((4, ROWS, D), F32),
+                pltpu.VMEM((8, ROWS, ROWS), BF16),
                 dma((2, 4, 4)), dma((2, 4, 4)), dma((2, 2, 5)), dma((2, 2, 5)),
                 dma((12,)), dma((12,)), dma((12,)), dma((12,)),
                 dma((4, 4)), dma((4, 4)),

time: 90.6 us -> 90.6 us (level)
  no operation moved by 1% of the time
where the time goes in v5:
time: 90.6 us; the launch traced here: 90.5 us
  Pallas kernels  88.4 us (98%)
  between operations  2.09 us (2%)
    pallas_call x1, Pallas kernels, shards(): pl.pallas_call(kernel, out_shape=(out, out, out), in_specs=[vm] * 8, out_...  86.1 us
    pallas_call x1, Pallas kernels, shards(): pl.pallas_call(place_out, out_shape=(out, out, out), in_specs=[anywhere]...  2.32 us

profile of v5, /device:TPU:1, one launch (start us, length us, event | category | flops | bytes accessed | tf_op | source)
XLA Modules:
  0.0 90.5 jit_solution(9541048868264758953)
XLA Ops:
  1.9 86.1 %shard_map.103 = (f32[128,1152]{1,0:T(8,128)}, f32[128,1152]{1,0:T(8,128)}, f32[128,1152]{1,0:T(8,128)}) custom-call(f32[1,1]{1,0:T(1,128)} %bitcast.5.ls_ref, f32[1,1]{1,0:T(1,128)} %bitcast.6.bias_ref, bf16[128,1152]{1,0:T(8,128)(2,1)} %images.1, bf16[128,1152]{1,0:T(8,128)(2,1)} %texts.1, bf16[128,1152]{1,0:T(8,128)(2,1)} %cache.1, s32[4,128]{1,0:T(4,128)} %bitcast.7, ...), custom_call_target="tpu_custom_call" | custom-call | flops 16999999488 | bytes 4000000 | tf_op jit(solution)/shard_map/pallas_call | solution.py:498
  88.0 2.3 %shard_map.104 = (f32[128,1152]{1,0:T(8,128)}, f32[128,1152]{1,0:T(8,128)}, f32[128,1152]{1,0:T(8,128)}) custom-call(f32[128,1152]{1,0:T(8,128)} %get-tuple-element.6.a, f32[128,1152]{1,0:T(8,128)} %get-tuple-element.7.b, f32[128,1152]{1,0:T(8,128)} %get-tuple-element.8.c), custom_call_target="tpu_custom_call" | custom-call | tf_op jit(solution)/shard_map/pallas_call | solution.py:540
